TPU v7x, 256 devices: a whole 4x4x8 slice. The times are simulated.
256 devices in a mesh: gx: 4 (over x), gy: 8 (over z), gz: 8 (over y, core).
Axes of the slice: x: 4, y: 4, z: 8, core: 2. Of those that a mesh axis runs over, the one named last changes fastest.
Arguments:
- multipoles: bfloat16 [65536, 256], P(('gx', 'gy', 'gz')), may hold values from -6 to 6
- translations: bfloat16 [16, 256, 256], replicated, may hold values from -0.09375 to 0.09375
- send_index: int32 [256, 256, 2], P(('gx', 'gy', 'gz')), may hold values from 0 to 255
- far_slots: int32 [65536, 16], P(('gx', 'gy', 'gz')), may hold values from 0 to 511
- far_types: int32 [65536, 16], P(('gx', 'gy', 'gz')), may hold values from 0 to 15
- near_list: int32 [65536, 8], P(('gx', 'gy', 'gz')), may hold values from 0 to 287
- particles: float32 [65536, 6, 128], P(('gx', 'gy', 'gz')), may hold values from -4 to 4
Outputs:
- local_expansions: float32 [65536, 256], P(('gx', 'gy', 'gz'))
- velocities: float32 [65536, 3, 128], P(('gx', 'gy', 'gz'))
All inputs are finite; a program needn't handle non-finite values.
Results may differ from a plain program's by a relative error of at most 0.0024.
Values may be sent and summed in bfloat16 or wider, within the bound.
No kernel may reach another device: no remote copies, remote signals or barrier semaphores. Data moves between devices by JAX's collectives and lax.ppermute only.
A program may use at most 64 MiB of HBM per device.

v0:
```python
import math

import jax
import jax.numpy as jnp
from jax import lax
from jax.sharding import PartitionSpec as P

Q = 256
P_SIZE = 128
NT = 16
NN = 8
CAP = 2
HALO = 16


EPS2 = 0.25


def extended_2(x, sides, width):
    for axis, dim in sides:
        devices, length = (lax.axis_size(axis), x.shape[dim])
        up = [(i, (i + 1) % devices) for i in range(devices - 1)]
        down = [(j, i) for i, j in up]
        last = lax.slice_in_dim(x, length - width, length, axis=dim)
        leading = lax.slice_in_dim(x, 0, width, axis=dim)
        before = lax.ppermute(last, axis, up)
        after = lax.ppermute(leading, axis, down)
        x = jnp.concatenate([before, x, after], axis=dim)
    return x


def stokes_pairs(targets, sources):
    d0 = targets[:, 0, :, None] - sources[:, 0, None, :]
    d1 = targets[:, 1, :, None] - sources[:, 1, None, :]
    d2 = targets[:, 2, :, None] - sources[:, 2, None, :]
    f0 = sources[:, 3, None, :]
    f1 = sources[:, 4, None, :]
    f2 = sources[:, 5, None, :]
    dist2 = d0 * d0 + d1 * d1 + d2 * d2
    inner = d0 * f0 + d1 * f1 + d2 * f2
    weight = (dist2 + EPS2) ** (-1.5)
    near = dist2 + 2.0 * EPS2
    u0 = jnp.sum((f0 * near + d0 * inner) * weight, axis=2)
    u1 = jnp.sum((f1 * near + d1 * inner) * weight, axis=2)
    u2 = jnp.sum((f2 * near + d2 * inner) * weight, axis=2)
    return jnp.stack([u0, u1, u2], axis=1)


def body(multipoles, translations, send_index, far_slots, far_types, near_list, particles):
    leaf_count = multipoles.shape[0]
    depth = lax.axis_size("gz")
    devices_all = send_index.shape[1]
    planes = devices_all // depth
    outgoing = multipoles[send_index[0]]
    outgoing = outgoing.reshape(planes, depth, CAP, Q)
    incoming = lax.all_to_all(
        lax.all_to_all(outgoing, ("gx", "gy"), split_axis=0, concat_axis=0, tiled=True),
        "gz",
        split_axis=1,
        concat_axis=1,
        tiled=True,
    )
    incoming = incoming.reshape(devices_all * CAP, Q)
    rows = incoming[far_slots]
    onehot = (far_types[:, :, None] == jnp.arange(NT, dtype=jnp.int32)[None, None, :]).astype(
        jnp.bfloat16
    )
    summed = jnp.einsum("lnt,lnq->ltq", onehot, rows, preferred_element_type=jnp.float32).astype(
        jnp.bfloat16
    )
    expansion = jnp.einsum("ltq,tqp->lp", summed, translations, preferred_element_type=jnp.float32)
    extended = extended_2(particles, ((("gx", "gy", "gz"), 0),), HALO)
    group = math.gcd(leaf_count, 32)
    mine = particles.reshape(leaf_count // group, group, 6, P_SIZE)
    neighbours = near_list.reshape(leaf_count // group, group, NN)
    scale = 1.0 / (8.0 * jnp.pi)

    def per_group(pair):
        targets, index = pair
        total = jnp.zeros((group, 3, P_SIZE), jnp.float32)
        for entry in range(NN):
            total = total + stokes_pairs(targets, extended[index[:, entry]])
        return total * scale

    speeds = lax.map(per_group, (mine, neighbours)).reshape(leaf_count, 3, P_SIZE)
    return (expansion, speeds)


def solution(mesh):
    placed = (
        P(("gx", "gy", "gz"), None),
        P(),
        P(("gx", "gy", "gz"), None, None),
        P(("gx", "gy", "gz"), None),
        P(("gx", "gy", "gz"), None),
        P(("gx", "gy", "gz"), None),
        P(("gx", "gy", "gz"), None, None),
    )
    return jax.shard_map(
        body,
        mesh=mesh,
        in_specs=placed,
        out_specs=(P(("gx", "gy", "gz"), None), P(("gx", "gy", "gz"), None, None)),
        check_vma=False,
    )
```

profile of v0, /device:TPU:1, one launch (start us, length us, event | category | flops | bytes accessed | tf_op | source)
XLA Modules:
  0.0 513.3 jit_solution(14394346341178255156)
XLA Ops:
  5.1 11.9 %all-to-all-start = ((bf16[32,8,2,256]{3,2,1,0:T(2,128)(2,1)}), bf16[32,8,2,256]{3,2,1,0:T(2,128)(2,1)S(1)}, u32[]{:S(2)}, u32[]{:S(2)}) async-start(bf16[32,8,2,256]{3,2,1,0:T(2,128)(2,1)} %reshape.411), calls=%async_computation | async-start | bytes 524288 | tf_op jit(solution)/shard_map/all_to_all | solution.py:57
  35.8 455.0 %while.10 = (s32[]{:T(128)}, f32[8,32,3,128]{3,1,0,2:T(8,128)}, s32[8,32,8]{1,0,2:T(8,128)}, f32[288,6,128]{2,1,0:T(8,128)S(1)}, f32[8,32,6,128]{3,1,0,2:T(8,128)}, /*index=5*/s32[]{:T(128)}) while((s32[]{:T(128)}, f32[8,32,3,128]{3,1,0,2:T(8,128)}, s32[8,32,8]{1,0,2:T(8,128)}, f32[288,6,128]{2,1,0:T(8,128)S(1)}, ...), condition=%wide.region_25.26_spmd, body=%wide.region_0.25_spmd.sunk | while | flops 126034688 | bytes 5956065 | solution.py:85
  53.0 11.0 %fusion.184 = (f32[32,128]{1,0:T(8,128)S(1)}, f32[32,128]{1,0:T(8,128)S(1)}, f32[32,128]{1,0:T(8,128)}, f32[32,128]{1,0:T(8,128)}, f32[32,128]{1,0:T(8,128)}, /*index=5*/f32[32,128]{1,0:T(8,128)}) fusion(f32[32,128]{1,0:T(8,128)} %bitcast.315, f32[32,128]{1,0:T(8,128)} %bitcast.311, f32[32,128]{1,0:T(8,128)} %bitcast.312, f32[32,128]{1,0:T(8,128)} %bitcast.313, ...), kind=kLoop, calls=%fused_computation.133.clone.1 | loop fusion | flops 31432704 | bytes 344064 | tf_op jit(solution)/shard_map/while/body/eval_jaxpr/reduce_sum | solution.py:43
  67.5 11.1 %fusion.187 = (f32[32,128]{1,0:T(8,128)}, f32[32,128]{1,0:T(8,128)}, f32[32,128]{1,0:T(8,128)}, f32[32,128]{1,0:T(8,128)}, f32[32,128]{1,0:T(8,128)}, /*index=5*/f32[32,128]{1,0:T(8,128)}) fusion(f32[32,128]{1,0:T(8,128)} %bitcast.321, f32[32,128]{1,0:T(8,128)} %bitcast.317, f32[32,128]{1,0:T(8,128)} %bitcast.318, f32[32,128]{1,0:T(8,128)} %bitcast.319, ...), kind=kLoop, calls=%fused_computation.163.clone.1 | loop fusion | flops 31432704 | bytes 344064 | tf_op jit(solution)/shard_map/while/body/eval_jaxpr/reduce_sum | solution.py:43
  81.5 10.4 %fusion.190 = (f32[32,128]{1,0:T(8,128)S(1)}, f32[32,128]{1,0:T(8,128)S(1)}, f32[32,128]{1,0:T(8,128)S(1)}, f32[32,128]{1,0:T(8,128)S(1)}, f32[32,128]{1,0:T(8,128)S(1)}, /*index=5*/f32[32,128]{1,0:T(8,128)S(1)}) fusion(f32[32,128]{1,0:T(8,128)} %bitcast.309, f32[32,128]{1,0:T(8,128)} %bitcast.305, f32[32,128]{1,0:T(8,128)} %bitcast.306, ...), kind=kLoop, calls=%fused_computation.193.clone.1 | loop fusion | flops 31432704 | bytes 344064 | tf_op jit(solution)/shard_map/while/body/eval_jaxpr/reduce_sum | solution.py:43
  109.9 11.0 %fusion.184 = (f32[32,128]{1,0:T(8,128)S(1)}, f32[32,128]{1,0:T(8,128)S(1)}, f32[32,128]{1,0:T(8,128)}, f32[32,128]{1,0:T(8,128)}, f32[32,128]{1,0:T(8,128)}, /*index=5*/f32[32,128]{1,0:T(8,128)}) fusion(f32[32,128]{1,0:T(8,128)} %bitcast.315, f32[32,128]{1,0:T(8,128)} %bitcast.311, f32[32,128]{1,0:T(8,128)} %bitcast.312, f32[32,128]{1,0:T(8,128)} %bitcast.313, ...), kind=kLoop, calls=%fused_computation.133.clone.1 | loop fusion | flops 31432704 | bytes 344064 | tf_op jit(solution)/shard_map/while/body/eval_jaxpr/reduce_sum | solution.py:43
  124.4 11.1 %fusion.187 = (f32[32,128]{1,0:T(8,128)}, f32[32,128]{1,0:T(8,128)}, f32[32,128]{1,0:T(8,128)}, f32[32,128]{1,0:T(8,128)}, f32[32,128]{1,0:T(8,128)}, /*index=5*/f32[32,128]{1,0:T(8,128)}) fusion(f32[32,128]{1,0:T(8,128)} %bitcast.321, f32[32,128]{1,0:T(8,128)} %bitcast.317, f32[32,128]{1,0:T(8,128)} %bitcast.318, f32[32,128]{1,0:T(8,128)} %bitcast.319, ...), kind=kLoop, calls=%fused_computation.163.clone.1 | loop fusion | flops 31432704 | bytes 344064 | tf_op jit(solution)/shard_map/while/body/eval_jaxpr/reduce_sum | solution.py:43
  138.4 10.4 %fusion.190 = (f32[32,128]{1,0:T(8,128)S(1)}, f32[32,128]{1,0:T(8,128)S(1)}, f32[32,128]{1,0:T(8,128)S(1)}, f32[32,128]{1,0:T(8,128)S(1)}, f32[32,128]{1,0:T(8,128)S(1)}, /*index=5*/f32[32,128]{1,0:T(8,128)S(1)}) fusion(f32[32,128]{1,0:T(8,128)} %bitcast.309, f32[32,128]{1,0:T(8,128)} %bitcast.305, f32[32,128]{1,0:T(8,128)} %bitcast.306, ...), kind=kLoop, calls=%fused_computation.193.clone.1 | loop fusion | flops 31432704 | bytes 344064 | tf_op jit(solution)/shard_map/while/body/eval_jaxpr/reduce_sum | solution.py:43
  166.7 11.0 %fusion.184 = (f32[32,128]{1,0:T(8,128)S(1)}, f32[32,128]{1,0:T(8,128)S(1)}, f32[32,128]{1,0:T(8,128)}, f32[32,128]{1,0:T(8,128)}, f32[32,128]{1,0:T(8,128)}, /*index=5*/f32[32,128]{1,0:T(8,128)}) fusion(f32[32,128]{1,0:T(8,128)} %bitcast.315, f32[32,128]{1,0:T(8,128)} %bitcast.311, f32[32,128]{1,0:T(8,128)} %bitcast.312, f32[32,128]{1,0:T(8,128)} %bitcast.313, ...), kind=kLoop, calls=%fused_computation.133.clone.1 | loop fusion | flops 31432704 | bytes 344064 | tf_op jit(solution)/shard_map/while/body/eval_jaxpr/reduce_sum | solution.py:43
  181.3 11.1 %fusion.187 = (f32[32,128]{1,0:T(8,128)}, f32[32,128]{1,0:T(8,128)}, f32[32,128]{1,0:T(8,128)}, f32[32,128]{1,0:T(8,128)}, f32[32,128]{1,0:T(8,128)}, /*index=5*/f32[32,128]{1,0:T(8,128)}) fusion(f32[32,128]{1,0:T(8,128)} %bitcast.321, f32[32,128]{1,0:T(8,128)} %bitcast.317, f32[32,128]{1,0:T(8,128)} %bitcast.318, f32[32,128]{1,0:T(8,128)} %bitcast.319, ...), kind=kLoop, calls=%fused_computation.163.clone.1 | loop fusion | flops 31432704 | bytes 344064 | tf_op jit(solution)/shard_map/while/body/eval_jaxpr/reduce_sum | solution.py:43
  195.2 10.4 %fusion.190 = (f32[32,128]{1,0:T(8,128)S(1)}, f32[32,128]{1,0:T(8,128)S(1)}, f32[32,128]{1,0:T(8,128)S(1)}, f32[32,128]{1,0:T(8,128)S(1)}, f32[32,128]{1,0:T(8,128)S(1)}, /*index=5*/f32[32,128]{1,0:T(8,128)S(1)}) fusion(f32[32,128]{1,0:T(8,128)} %bitcast.309, f32[32,128]{1,0:T(8,128)} %bitcast.305, f32[32,128]{1,0:T(8,128)} %bitcast.306, ...), kind=kLoop, calls=%fused_computation.193.clone.1 | loop fusion | flops 31432704 | bytes 344064 | tf_op jit(solution)/shard_map/while/body/eval_jaxpr/reduce_sum | solution.py:43
  223.6 11.0 %fusion.184 = (f32[32,128]{1,0:T(8,128)S(1)}, f32[32,128]{1,0:T(8,128)S(1)}, f32[32,128]{1,0:T(8,128)}, f32[32,128]{1,0:T(8,128)}, f32[32,128]{1,0:T(8,128)}, /*index=5*/f32[32,128]{1,0:T(8,128)}) fusion(f32[32,128]{1,0:T(8,128)} %bitcast.315, f32[32,128]{1,0:T(8,128)} %bitcast.311, f32[32,128]{1,0:T(8,128)} %bitcast.312, f32[32,128]{1,0:T(8,128)} %bitcast.313, ...), kind=kLoop, calls=%fused_computation.133.clone.1 | loop fusion | flops 31432704 | bytes 344064 | tf_op jit(solution)/shard_map/while/body/eval_jaxpr/reduce_sum | solution.py:43
  238.1 11.1 %fusion.187 = (f32[32,128]{1,0:T(8,128)}, f32[32,128]{1,0:T(8,128)}, f32[32,128]{1,0:T(8,128)}, f32[32,128]{1,0:T(8,128)}, f32[32,128]{1,0:T(8,128)}, /*index=5*/f32[32,128]{1,0:T(8,128)}) fusion(f32[32,128]{1,0:T(8,128)} %bitcast.321, f32[32,128]{1,0:T(8,128)} %bitcast.317, f32[32,128]{1,0:T(8,128)} %bitcast.318, f32[32,128]{1,0:T(8,128)} %bitcast.319, ...), kind=kLoop, calls=%fused_computation.163.clone.1 | loop fusion | flops 31432704 | bytes 344064 | tf_op jit(solution)/shard_map/while/body/eval_jaxpr/reduce_sum | solution.py:43
  280.5 11.0 %fusion.184 = (f32[32,128]{1,0:T(8,128)S(1)}, f32[32,128]{1,0:T(8,128)S(1)}, f32[32,128]{1,0:T(8,128)}, f32[32,128]{1,0:T(8,128)}, f32[32,128]{1,0:T(8,128)}, /*index=5*/f32[32,128]{1,0:T(8,128)}) fusion(f32[32,128]{1,0:T(8,128)} %bitcast.315, f32[32,128]{1,0:T(8,128)} %bitcast.311, f32[32,128]{1,0:T(8,128)} %bitcast.312, f32[32,128]{1,0:T(8,128)} %bitcast.313, ...), kind=kLoop, calls=%fused_computation.133.clone.1 | loop fusion | flops 31432704 | bytes 344064 | tf_op jit(solution)/shard_map/while/body/eval_jaxpr/reduce_sum | solution.py:43
  295.0 11.1 %fusion.187 = (f32[32,128]{1,0:T(8,128)}, f32[32,128]{1,0:T(8,128)}, f32[32,128]{1,0:T(8,128)}, f32[32,128]{1,0:T(8,128)}, f32[32,128]{1,0:T(8,128)}, /*index=5*/f32[32,128]{1,0:T(8,128)}) fusion(f32[32,128]{1,0:T(8,128)} %bitcast.321, f32[32,128]{1,0:T(8,128)} %bitcast.317, f32[32,128]{1,0:T(8,128)} %bitcast.318, f32[32,128]{1,0:T(8,128)} %bitcast.319, ...), kind=kLoop, calls=%fused_computation.163.clone.1 | loop fusion | flops 31432704 | bytes 344064 | tf_op jit(solution)/shard_map/while/body/eval_jaxpr/reduce_sum | solution.py:43
  337.4 11.0 %fusion.184 = (f32[32,128]{1,0:T(8,128)S(1)}, f32[32,128]{1,0:T(8,128)S(1)}, f32[32,128]{1,0:T(8,128)}, f32[32,128]{1,0:T(8,128)}, f32[32,128]{1,0:T(8,128)}, /*index=5*/f32[32,128]{1,0:T(8,128)}) fusion(f32[32,128]{1,0:T(8,128)} %bitcast.315, f32[32,128]{1,0:T(8,128)} %bitcast.311, f32[32,128]{1,0:T(8,128)} %bitcast.312, f32[32,128]{1,0:T(8,128)} %bitcast.313, ...), kind=kLoop, calls=%fused_computation.133.clone.1 | loop fusion | flops 31432704 | bytes 344064 | tf_op jit(solution)/shard_map/while/body/eval_jaxpr/reduce_sum | solution.py:43
  351.9 11.1 %fusion.187 = (f32[32,128]{1,0:T(8,128)}, f32[32,128]{1,0:T(8,128)}, f32[32,128]{1,0:T(8,128)}, f32[32,128]{1,0:T(8,128)}, f32[32,128]{1,0:T(8,128)}, /*index=5*/f32[32,128]{1,0:T(8,128)}) fusion(f32[32,128]{1,0:T(8,128)} %bitcast.321, f32[32,128]{1,0:T(8,128)} %bitcast.317, f32[32,128]{1,0:T(8,128)} %bitcast.318, f32[32,128]{1,0:T(8,128)} %bitcast.319, ...), kind=kLoop, calls=%fused_computation.163.clone.1 | loop fusion | flops 31432704 | bytes 344064 | tf_op jit(solution)/shard_map/while/body/eval_jaxpr/reduce_sum | solution.py:43
  394.2 11.0 %fusion.184 = (f32[32,128]{1,0:T(8,128)S(1)}, f32[32,128]{1,0:T(8,128)S(1)}, f32[32,128]{1,0:T(8,128)}, f32[32,128]{1,0:T(8,128)}, f32[32,128]{1,0:T(8,128)}, /*index=5*/f32[32,128]{1,0:T(8,128)}) fusion(f32[32,128]{1,0:T(8,128)} %bitcast.315, f32[32,128]{1,0:T(8,128)} %bitcast.311, f32[32,128]{1,0:T(8,128)} %bitcast.312, f32[32,128]{1,0:T(8,128)} %bitcast.313, ...), kind=kLoop, calls=%fused_computation.133.clone.1 | loop fusion | flops 31432704 | bytes 344064 | tf_op jit(solution)/shard_map/while/body/eval_jaxpr/reduce_sum | solution.py:43
  408.8 11.1 %fusion.187 = (f32[32,128]{1,0:T(8,128)}, f32[32,128]{1,0:T(8,128)}, f32[32,128]{1,0:T(8,128)}, f32[32,128]{1,0:T(8,128)}, f32[32,128]{1,0:T(8,128)}, /*index=5*/f32[32,128]{1,0:T(8,128)}) fusion(f32[32,128]{1,0:T(8,128)} %bitcast.321, f32[32,128]{1,0:T(8,128)} %bitcast.317, f32[32,128]{1,0:T(8,128)} %bitcast.318, f32[32,128]{1,0:T(8,128)} %bitcast.319, ...), kind=kLoop, calls=%fused_computation.163.clone.1 | loop fusion | flops 31432704 | bytes 344064 | tf_op jit(solution)/shard_map/while/body/eval_jaxpr/reduce_sum | solution.py:43
  422.7 10.4 %fusion.190 = (f32[32,128]{1,0:T(8,128)S(1)}, f32[32,128]{1,0:T(8,128)S(1)}, f32[32,128]{1,0:T(8,128)S(1)}, f32[32,128]{1,0:T(8,128)S(1)}, f32[32,128]{1,0:T(8,128)S(1)}, /*index=5*/f32[32,128]{1,0:T(8,128)S(1)}) fusion(f32[32,128]{1,0:T(8,128)} %bitcast.309, f32[32,128]{1,0:T(8,128)} %bitcast.305, f32[32,128]{1,0:T(8,128)} %bitcast.306, ...), kind=kLoop, calls=%fused_computation.193.clone.1 | loop fusion | flops 31432704 | bytes 344064 | tf_op jit(solution)/shard_map/while/body/eval_jaxpr/reduce_sum | solution.py:43
  451.1 11.0 %fusion.184 = (f32[32,128]{1,0:T(8,128)S(1)}, f32[32,128]{1,0:T(8,128)S(1)}, f32[32,128]{1,0:T(8,128)}, f32[32,128]{1,0:T(8,128)}, f32[32,128]{1,0:T(8,128)}, /*index=5*/f32[32,128]{1,0:T(8,128)}) fusion(f32[32,128]{1,0:T(8,128)} %bitcast.315, f32[32,128]{1,0:T(8,128)} %bitcast.311, f32[32,128]{1,0:T(8,128)} %bitcast.312, f32[32,128]{1,0:T(8,128)} %bitcast.313, ...), kind=kLoop, calls=%fused_computation.133.clone.1 | loop fusion | flops 31432704 | bytes 344064 | tf_op jit(solution)/shard_map/while/body/eval_jaxpr/reduce_sum | solution.py:43
  465.6 11.1 %fusion.187 = (f32[32,128]{1,0:T(8,128)}, f32[32,128]{1,0:T(8,128)}, f32[32,128]{1,0:T(8,128)}, f32[32,128]{1,0:T(8,128)}, f32[32,128]{1,0:T(8,128)}, /*index=5*/f32[32,128]{1,0:T(8,128)}) fusion(f32[32,128]{1,0:T(8,128)} %bitcast.321, f32[32,128]{1,0:T(8,128)} %bitcast.317, f32[32,128]{1,0:T(8,128)} %bitcast.318, f32[32,128]{1,0:T(8,128)} %bitcast.319, ...), kind=kLoop, calls=%fused_computation.163.clone.1 | loop fusion | flops 31432704 | bytes 344064 | tf_op jit(solution)/shard_map/while/body/eval_jaxpr/reduce_sum | solution.py:43
  479.6 10.4 %fusion.190 = (f32[32,128]{1,0:T(8,128)S(1)}, f32[32,128]{1,0:T(8,128)S(1)}, f32[32,128]{1,0:T(8,128)S(1)}, f32[32,128]{1,0:T(8,128)S(1)}, f32[32,128]{1,0:T(8,128)S(1)}, /*index=5*/f32[32,128]{1,0:T(8,128)S(1)}) fusion(f32[32,128]{1,0:T(8,128)} %bitcast.309, f32[32,128]{1,0:T(8,128)} %bitcast.305, f32[32,128]{1,0:T(8,128)} %bitcast.306, ...), kind=kLoop, calls=%fused_computation.193.clone.1 | loop fusion | flops 31432704 | bytes 344064 | tf_op jit(solution)/shard_map/while/body/eval_jaxpr/reduce_sum | solution.py:43
  492.0 16.9 %gather_fusion.9 = bf16[4096,256]{1,0:T(8,128)(2,1)} fusion(bf16[512,256]{1,0:T(8,128)(2,1)S(1)} %reshape.412, s32[4096]{0:T(1024)S(1)} %broadcast_clamp_fusion), kind=kCustom, calls=%fused_computation.9 | custom fusion | bytes 4210688 | tf_op jit(solution)/shard_map/gather | solution.py:64
  (479 shorter events, 252.2 us)
Async XLA Ops:
  0.6 510.6 %copy-start = (bf16[16,256,256]{2,1,0:T(8,128)(2,1)S(1)}, bf16[16,256,256]{2,1,0:T(8,128)(2,1)}, u32[]{:S(2)}) copy-start(bf16[16,256,256]{2,1,0:T(8,128)(2,1)} %param.10) | copy-start | bytes 6291460
  0.6 16.4 %copy-start.2 = (f32[256,6,128]{2,0,1:T(8,128)S(1)}, f32[256,6,128]{2,0,1:T(8,128)}, u32[]{:S(2)}) copy-start(f32[256,6,128]{2,0,1:T(8,128)} %param.15) | copy-start | bytes 2359300
  4.3 20.2 %copy-start.20 = (s32[256,16]{0,1:T(8,128)S(1)}, s32[256,16]{0,1:T(8,128)}, u32[]{:S(2)}) copy-start(s32[256,16]{0,1:T(8,128)} %param.12) | copy-start | bytes 49156
  4.3 20.4 %copy-start.19 = (s32[256,16]{0,1:T(8,128)S(1)}, s32[256,16]{0,1:T(8,128)}, u32[]{:S(2)}) copy-start(s32[256,16]{0,1:T(8,128)} %param.13) | copy-start | bytes 49156
  4.3 21.2 %copy-start.21 = (s32[256,8]{0,1:T(8,128)S(1)}, s32[256,8]{0,1:T(8,128)}, u32[]{:S(2)}) copy-start(s32[256,8]{0,1:T(8,128)} %param.14) | copy-start | bytes 24580
  5.1 23.0 %all-to-all-start = ((bf16[32,8,2,256]{3,2,1,0:T(2,128)(2,1)}), bf16[32,8,2,256]{3,2,1,0:T(2,128)(2,1)S(1)}, u32[]{:S(2)}, u32[]{:S(2)}) async-start(bf16[32,8,2,256]{3,2,1,0:T(2,128)(2,1)} %reshape.411), calls=%async_computation | async-start | bytes 524288 | tf_op jit(solution)/shard_map/all_to_all | solution.py:57
  18.5 7.7 %collective-permute-start.1 = (f32[16,6,128]{2,1,0:T(8,128)S(1)}, f32[16,6,128]{2,1,0:T(8,128)S(1)}, u32[]{:S(2)}, u32[]{:S(2)}) collective-permute-start(f32[16,6,128]{2,1,0:T(8,128)S(1)} %get-tuple-element.169), channel_id=1, source_target_pairs={{1,0},{2,1},{3,2},{4,3},{5,4},{6,5},{7,6},{8,7},{9,8},{10,9},{11,1... | collective-permute-start | bytes 147464 | tf_op jit(solution)/shard_map/ppermute | solution.py:27
  21.4 5.4 %collective-permute-start = (f32[16,6,128]{2,1,0:T(8,128)S(1)}, f32[16,6,128]{2,1,0:T(8,128)}, u32[]{:S(2)}, u32[]{:S(2)}) collective-permute-start(f32[16,6,128]{2,1,0:T(8,128)S(1)} %get-tuple-element.168), channel_id=1, source_target_pairs={{0,1},{1,2},{2,3},{3,4},{4,5},{5,6},{6,7},{7,8},{8,9},{9,10},{10,1... | collective-permute-start | bytes 147464 | tf_op jit(solution)/shard_map/ppermute | solution.py:26
  29.1 461.7 %all-to-all-start.1 = ((bf16[32,8,2,256]{3,2,0,1:T(2,128)(2,1)}), bf16[32,8,2,256]{3,2,0,1:T(2,128)(2,1)}, u32[]{:S(2)}, u32[]{:S(2)}) async-start(bf16[32,8,2,256]{3,2,0,1:T(2,128)(2,1)} %copy.61), calls=%async_computation.1 | async-start | bytes 524288 | tf_op jit(solution)/shard_map/all_to_all | solution.py:56
  67.4 11.2 %copy-start.15 = (s32[32]{0:T(128)S(1)}, s32[32]{0:T(128)}, u32[]{:S(2)}) copy-start(s32[32]{0:T(128)} %get-tuple-element.362) | copy-start | bytes 388 | tf_op jit(solution)/shard_map/while
  67.4 11.1 %copy-start.16 = (s32[32]{0:T(128)S(1)}, s32[32]{0:T(128)}, u32[]{:S(2)}) copy-start(s32[32]{0:T(128)} %get-tuple-element.361) | copy-start | bytes 388 | tf_op jit(solution)/shard_map/while
  124.3 11.2 %copy-start.15 = (s32[32]{0:T(128)S(1)}, s32[32]{0:T(128)}, u32[]{:S(2)}) copy-start(s32[32]{0:T(128)} %get-tuple-element.362) | copy-start | bytes 388 | tf_op jit(solution)/shard_map/while
  124.3 11.1 %copy-start.16 = (s32[32]{0:T(128)S(1)}, s32[32]{0:T(128)}, u32[]{:S(2)}) copy-start(s32[32]{0:T(128)} %get-tuple-element.361) | copy-start | bytes 388 | tf_op jit(solution)/shard_map/while
  181.2 11.2 %copy-start.15 = (s32[32]{0:T(128)S(1)}, s32[32]{0:T(128)}, u32[]{:S(2)}) copy-start(s32[32]{0:T(128)} %get-tuple-element.362) | copy-start | bytes 388 | tf_op jit(solution)/shard_map/while
  181.2 11.1 %copy-start.16 = (s32[32]{0:T(128)S(1)}, s32[32]{0:T(128)}, u32[]{:S(2)}) copy-start(s32[32]{0:T(128)} %get-tuple-element.361) | copy-start | bytes 388 | tf_op jit(solution)/shard_map/while
  238.0 11.2 %copy-start.15 = (s32[32]{0:T(128)S(1)}, s32[32]{0:T(128)}, u32[]{:S(2)}) copy-start(s32[32]{0:T(128)} %get-tuple-element.362) | copy-start | bytes 388 | tf_op jit(solution)/shard_map/while
  238.0 11.1 %copy-start.16 = (s32[32]{0:T(128)S(1)}, s32[32]{0:T(128)}, u32[]{:S(2)}) copy-start(s32[32]{0:T(128)} %get-tuple-element.361) | copy-start | bytes 388 | tf_op jit(solution)/shard_map/while
  294.9 11.2 %copy-start.15 = (s32[32]{0:T(128)S(1)}, s32[32]{0:T(128)}, u32[]{:S(2)}) copy-start(s32[32]{0:T(128)} %get-tuple-element.362) | copy-start | bytes 388 | tf_op jit(solution)/shard_map/while
  294.9 11.1 %copy-start.16 = (s32[32]{0:T(128)S(1)}, s32[32]{0:T(128)}, u32[]{:S(2)}) copy-start(s32[32]{0:T(128)} %get-tuple-element.361) | copy-start | bytes 388 | tf_op jit(solution)/shard_map/while
  351.8 11.2 %copy-start.15 = (s32[32]{0:T(128)S(1)}, s32[32]{0:T(128)}, u32[]{:S(2)}) copy-start(s32[32]{0:T(128)} %get-tuple-element.362) | copy-start | bytes 388 | tf_op jit(solution)/shard_map/while
  351.8 11.1 %copy-start.16 = (s32[32]{0:T(128)S(1)}, s32[32]{0:T(128)}, u32[]{:S(2)}) copy-start(s32[32]{0:T(128)} %get-tuple-element.361) | copy-start | bytes 388 | tf_op jit(solution)/shard_map/while
  408.7 11.2 %copy-start.15 = (s32[32]{0:T(128)S(1)}, s32[32]{0:T(128)}, u32[]{:S(2)}) copy-start(s32[32]{0:T(128)} %get-tuple-element.362) | copy-start | bytes 388 | tf_op jit(solution)/shard_map/while
  465.5 11.2 %copy-start.15 = (s32[32]{0:T(128)S(1)}, s32[32]{0:T(128)}, u32[]{:S(2)}) copy-start(s32[32]{0:T(128)} %get-tuple-element.362) | copy-start | bytes 388 | tf_op jit(solution)/shard_map/while
  492.0 16.9 %copy-start.3 = (s32[256,16]{1,0:T(8,128)S(1)}, s32[256,16]{1,0:T(8,128)}, u32[]{:S(2)}) copy-start(s32[256,16]{1,0:T(8,128)} %copy.59) | copy-start | bytes 49156
  (100 other events, 1038.5 us)
where the time goes:
time: 522 us; the launch traced here: 513 us
  other arithmetic  370 us (71%)
  local copies, waits for them, and re-layouts  111 us (21%)
  starting transfers between devices  24.5 us (5%)
    reduce_sum x32, other arithmetic, stokes_pairs(): u0 = jnp.sum((f0 * near + d0 * inner) * weight, axis=2)  343 us
    gather x64, local copies, waits for them, and re-layouts, per_group(): total = total + stokes_pairs(targets, extended[index[:, entry]])  41.3 us
    slice x32, local copies, waits for them, and re-layouts, stokes_pairs(): f0 = sources[:, 3, None, :]  22.1 us
    gather x1, local copies, waits for them, and re-layouts, body(): rows = incoming[far_slots]  16.9 us
    gather x32, other arithmetic, per_group(): total = total + stokes_pairs(targets, extended[index[:, entry]])  15.1 us
    all_to_all x1, starting transfers between devices, body(): lax.all_to_all(outgoing, ('gx', 'gy'), split_axis=0, concat_axis=0, tiled...  11.9 us
  transfers between devices with their start and end apart: 4, of which 0 were waited for; matrix products, arithmetic and copies ran while one was open for 89% of the time, Pallas kernels for 0%

commit v1 on v0

v1 whole, which is shorter than its diff:
```python
import functools
import math

import jax
import jax.numpy as jnp
from jax import lax
from jax.experimental import pallas as pl
from jax.experimental.pallas import tpu as pltpu
from jax.sharding import PartitionSpec as P

Q = 256
P_SIZE = 128
NT = 16
NN = 8
CAP = 2
HALO = 16
EPS2 = 0.25
NLF = 256
NE = NLF + 2 * HALO
UNROLL = 4
bf = jnp.bfloat16
f32 = jnp.float32


def split3(v):
    a=v.astype(bf).astype(f32); r=v-a
    b=r.astype(bf).astype(f32)
    return a,b,r-b

def near_kernel(near_ref, before_ref, mine_ref, after_ref, out_ref, ext, tgt, bt, gb, wa, wb, acc, *, U):
    rows=lax.broadcasted_iota(jnp.int32,(8,128),0)
    lane=lax.broadcasted_iota(jnp.int32,(1,128),1)
    z8=jnp.zeros((8,128),f32)
    ext[0:8,:]=z8
    ext[(NE+1)*8:(NE+2)*8,:]=z8
    def cp(ref,base,n):
        def one(e,_):
            r0=pl.multiple_of((base+e+1)*8,8)
            ext[pl.ds(r0,8),:]=z8
            ext[pl.ds(r0,6),:]=ref[e]
            return 0
        lax.fori_loop(0,n,one,0,unroll=8)
    cp(before_ref,0,16); cp(mine_ref,16,256); cp(after_ref,272,16)
    def bc(r): return jnp.broadcast_to(ext[pl.ds(r,1),:],(8,128))
    lo3=rows<3; lo6=rows<6; is6=rows==6
    def one(e):
        r0=(e+1)*8
        y=[bc(r0+c) for c in range(3)]; f=[bc(r0+3+c) for c in range(3)]
        Pt=ext[pl.ds(r0,8),:]; Pm=ext[pl.ds(r0+3,8),:]; Pq=ext[pl.ds(r0-3,8),:]
        n=y[0]*y[0]+y[1]*y[1]+y[2]*y[2]
        a=y[0]*f[0]+y[1]*f[1]+y[2]*f[2]
        t0=jnp.where(lo3,n*Pm+a*Pt,jnp.where(lo6,Pt,jnp.where(is6,a,y[2]*f[2])))
        t1=jnp.where(lo3,y[0]*Pm,jnp.where(lo6,y[1]*Pt,y[2]*Pq))
        t=jnp.concatenate([t0,t1],axis=0)
        g1,g2,g3=split3(t)
        gb[e]=jnp.concatenate([g1,g2,g3],axis=0).astype(bf)
        Q=jnp.where(lo3,Pt,Pq)
        q1,q2,q3=split3(Q)
        m=split3(n+EPS2)
        M=[jnp.where(is6,v,1.0) for v in m]
        src=jnp.concatenate([jnp.where(lo6,q1,M[0]),jnp.where(lo3,q1,jnp.where(lo6,q2,M[1])),jnp.where(lo3,q2,jnp.where(lo6,q3,M[2])),z8],axis=0)
        nn=split3(n)
        Nn=[jnp.where(is6,1.0,v) for v in nn]
        d1,d2,d3=-2.0*q1,-2.0*q2,-2.0*q3
        tg=jnp.concatenate([jnp.where(lo3,d1,jnp.where(lo6,d2,Nn[0])),jnp.where(lo3,d3,jnp.where(lo6,d1,Nn[1])),jnp.where(lo3,d2,jnp.where(lo6,d1,Nn[2])),z8],axis=0)
        tgt[e]=tg.astype(bf)
        return src
    def four(i,_):
        s=jnp.concatenate([one(i*4+v) for v in range(4)],axis=0)
        B=s.T.astype(bf)
        for v in range(4):
            bt[i*4+v]=jnp.where((lane>=32*v)&(lane<32*v+32),B,jnp.zeros((),bf))
        return 0
    lax.fori_loop(0,NE//4,four,0)
    Z=jnp.zeros((128,128),bf)
    def stage1(l,w,u):
        A=tgt[l+16]
        A4=jnp.concatenate([A,A,A,A],axis=0)
        R=jnp.concatenate([jnp.concatenate([A4,Z],axis=1),jnp.concatenate([Z,A4],axis=1)],axis=0)
        for p in range(NN//2):
            k1=near_ref[2*p,l]; k2=near_ref[2*p+1,l]
            L=jnp.concatenate([bt[k1],bt[k2]],axis=1)
            s=jnp.dot(L,R,preferred_element_type=f32)
            v=lax.rsqrt(s)
            w3=(v*v*v).astype(bf)
            w[u,p*256:p*256+128,:]=w3[:,:128]
            w[u,p*256+128:p*256+256,:]=w3[:,128:]
    def stage2(l,w,u):
        G=jnp.concatenate([gb[near_ref[k,l]] for k in range(NN)],axis=1)
        T=jnp.dot(G,w[u],preferred_element_type=f32)
        acc[pl.ds(pl.multiple_of(l*16,16),16),:]=T[0:16]+T[16:32]+T[32:48]
    for u in range(U): stage1(u,wa,u)
    def it(i,_):
        b=i*2*U
        for u in range(U):
            stage1(b+U+u,wb,u)
            stage2(b+u,wa,u)
        for u in range(U):
            stage1(jnp.minimum(b+2*U+u,NLF-1),wa,u)
            stage2(b+U+u,wb,u)
        return 0
    lax.fori_loop(0,NLF//(2*U),it,0)
    scale=1.0/(8.0*math.pi)
    def fin(g,_):
        x=[mine_ref[pl.ds(g*8,8),c,:] for c in range(3)]
        t=[acc[pl.ds(g*8*16+r,8,stride=16),:] for r in range(16)]
        n=x[0]*x[0]+x[1]*x[1]+x[2]*x[2]+2*EPS2
        N=t[0:3]; F=t[3:6]; A=t[6]
        Ym=[t[8:11],t[11:14],[t[14],t[15],t[7]]]
        xf=x[0]*F[0]+x[1]*F[1]+x[2]*F[2]-A
        for c in range(3):
            v=n*F[c]+N[c]+x[c]*xf
            for b in range(3):
                v=v-x[b]*(2.0*Ym[b][c]+Ym[c][b])
            out_ref[c,pl.ds(g*8,8),:]=v*scale
        return 0
    lax.fori_loop(0,32,fin,0)


def near(near_list, before, mine, after):
    return pl.pallas_call(
        functools.partial(near_kernel, U=UNROLL),
        out_shape=jax.ShapeDtypeStruct((3, NLF, P_SIZE), f32),
        in_specs=[pl.BlockSpec(memory_space=pltpu.SMEM)] + [pl.BlockSpec(memory_space=pltpu.VMEM)] * 3,
        out_specs=pl.BlockSpec(memory_space=pltpu.VMEM),
        scratch_shapes=[
            pltpu.VMEM(((NE + 2) * 8, 128), f32),
            pltpu.VMEM((NE, 32, 128), bf),
            pltpu.VMEM((NE, 128, 128), bf),
            pltpu.VMEM((NE, 48, 128), bf),
            pltpu.VMEM((UNROLL, 1024, 128), bf),
            pltpu.VMEM((UNROLL, 1024, 128), bf),
            pltpu.VMEM((NLF * 16, 128), f32),
        ],
        compiler_params=pltpu.CompilerParams(vmem_limit_bytes=48 * 2**20),
        cost_estimate=pl.CostEstimate(flops=60 * 10**9, bytes_accessed=2 * 10**6, transcendentals=33 * 10**6),
    )(near_list.T, before, mine, after)


def halo(x, axes):
    devices = lax.axis_size(axes)
    up = [(i, i + 1) for i in range(devices - 1)]
    down = [(j, i) for i, j in up]
    before = lax.ppermute(x[x.shape[0] - HALO :], axes, up)
    after = lax.ppermute(x[:HALO], axes, down)
    return before, after


def body(multipoles, translations, send_index, far_slots, far_types, near_list, particles):
    depth = lax.axis_size("gz")
    devices_all = send_index.shape[1]
    planes = devices_all // depth
    before, after = halo(particles, ("gx", "gy", "gz"))
    outgoing = multipoles[send_index[0]]
    outgoing = outgoing.reshape(planes, depth, CAP, Q)
    incoming = lax.all_to_all(
        lax.all_to_all(outgoing, ("gx", "gy"), split_axis=0, concat_axis=0, tiled=True),
        "gz",
        split_axis=1,
        concat_axis=1,
        tiled=True,
    )
    incoming = incoming.reshape(devices_all * CAP, Q)
    rows = incoming[far_slots]
    onehot = (far_types[:, :, None] == jnp.arange(NT, dtype=jnp.int32)[None, None, :]).astype(bf)
    summed = jnp.einsum("lnt,lnq->ltq", onehot, rows, preferred_element_type=f32).astype(bf)
    expansion = jnp.einsum("ltq,tqp->lp", summed, translations, preferred_element_type=f32)
    speeds = near(near_list, before, particles, after)
    return (expansion, jnp.transpose(speeds, (1, 0, 2)))


def solution(mesh):
    placed = (
        P(("gx", "gy", "gz"), None),
        P(),
        P(("gx", "gy", "gz"), None, None),
        P(("gx", "gy", "gz"), None),
        P(("gx", "gy", "gz"), None),
        P(("gx", "gy", "gz"), None),
        P(("gx", "gy", "gz"), None, None),
    )
    return jax.shard_map(
        body,
        mesh=mesh,
        in_specs=placed,
        out_specs=(P(("gx", "gy", "gz"), None), P(("gx", "gy", "gz"), None, None)),
        check_vma=False,
    )
```

time: 522 us -> 114 us (0.22); the launches traced: 513 us -> 113 us
  other arithmetic: 370 us -> 0.85 us
  local copies, waits for them, and re-layouts: 111 us -> 26.2 us
  Pallas kernels: 0 us -> 53.8 us
    reduce_sum x32 -> x0, other arithmetic: 343 us -> none  [stokes_pairs(): u0 = jnp.sum((f0 * near + d0 * inner) * weight, axis=2)]
    pallas_call x0 -> x1, Pallas kernels: none -> 53.8 us  [near(): pl.pallas_call(functools.partial(near_kernel, U=UNROLL), out_shape=jax.Sh...]
    gather x64 -> x0, local copies, waits for them, and re-layouts: 41.3 us -> none  [per_group(): total = total + stokes_pairs(targets, extended[index[:, entry]])]
    slice x65 -> x1, local copies, waits for them, and re-layouts: 24.4 us -> 0.64 us  [halo(): after = lax.ppermute(x[:HALO], axes, down)]
    gather x32 -> x0, other arithmetic: 15.1 us -> none  [per_group(): total = total + stokes_pairs(targets, extended[index[:, entry]])]
    squeeze x8 -> x0, local copies, waits for them, and re-layouts: 7.2 us -> none  [body(): lax.map(per_group, (mine, neighbours)).reshape(leaf_count, 3, P_SIZE)]
    dynamic_slice x8 -> x0, local copies, waits for them, and re-layouts: 6.11 us -> none  [body(): lax.map(per_group, (mine, neighbours)).reshape(leaf_count, 3, P_SIZE)]
    dynamic_update_slice x8 -> x0, other arithmetic: 5.31 us -> none  [body(): lax.map(per_group, (mine, neighbours)).reshape(leaf_count, 3, P_SIZE)]
  transfers between devices with their start and end apart: 4 -> 4, of which waited for: 0 -> 1; matrix products, arithmetic and copies ran while one was open for 89% -> 4% of each run, Pallas kernels for 0% -> 47%
where the time goes in v1:
time: 114 us; the launch traced here: 113 us
  Pallas kernels  53.8 us (47%)
  starting transfers between devices  26.3 us (23%)
  local copies, waits for them, and re-layouts  26.2 us (23%)
  matrix products  4.3 us (4%)
    pallas_call x1, Pallas kernels, near(): pl.pallas_call(functools.partial(near_kernel, U=UNROLL), out_shape=jax.Sh...  53.8 us
    gather x1, local copies, waits for them, and re-layouts, body(): rows = incoming[far_slots]  17 us
    all_to_all x1, starting transfers between devices, body(): lax.all_to_all(outgoing, ('gx', 'gy'), split_axis=0, concat_axis=0, tiled...  12.1 us
    all_to_all x1, starting transfers between devices, body(): lax.all_to_all(lax.all_to_all(outgoing, ('gx', 'gy'), split_axis=0, conca...  8.19 us
    ppermute x1, starting transfers between devices, halo(): before = lax.ppermute(x[x.shape[0] - HALO:], axes, up)  4.03 us
    gather x1, local copies, waits for them, and re-layouts, body(): outgoing = multipoles[send_index[0]]  2.48 us
    dot_general x1, matrix products, body(): jnp.einsum('lnt,lnq->ltq', onehot, rows, preferred_element_type=f32)  2.28 us
  transfers between devices with their start and end apart: 4, of which 1 were waited for; matrix products, arithmetic and copies ran while one was open for 4% of the time, Pallas kernels for 47%

profile of v1, /device:TPU:1, one launch (start us, length us, event | category | flops | bytes accessed | tf_op | source)
XLA Modules:
  0.0 113.3 jit_solution(7678749495631206155)
XLA Ops:
  0.6 0.0 copy-start
  0.6 0.8 compare_select_fusion.1
  1.5 0.1 copy.29
  1.6 0.1 reshape.43
  1.8 2.5 %gather_fusion = bf16[512,256]{1,0:T(8,128)(2,1)S(1)} fusion(bf16[256,256]{1,0:T(8,128)(2,1)} %param.7, s32[1024]{0:T(1024)S(1)} %pad_clamp_fusion), kind=kCustom, calls=%fused_computation | custom fusion | bytes 526336 | tf_op jit(solution)/shard_map/gather | solution.py:154
  4.3 0.0 copy-start.3
  4.3 0.8 reshape.39
  5.1 12.1 %all-to-all-start = ((bf16[32,8,2,256]{3,2,1,0:T(2,128)(2,1)}), bf16[32,8,2,256]{3,2,1,0:T(2,128)(2,1)}, u32[]{:S(2)}, u32[]{:S(2)}) async-start(bf16[32,8,2,256]{3,2,1,0:T(2,128)(2,1)} %reshape.39), calls=%async_computation | async-start | bytes 524288 | tf_op jit(solution)/shard_map/all_to_all | solution.py:157
  17.2 1.6 %copy.34.mine_ref = f32[256,6,128]{2,1,0:T(8,128)S(1)} copy(f32[256,6,128]{2,0,1:T(8,128)} %param.13) | data formatting | bytes 1572864 | tf_op args[6]
  18.9 0.6 fusion.8
  19.5 4.0 %collective-permute-start = (f32[16,6,128]{2,1,0:T(8,128)}, f32[16,6,128]{2,1,0:T(8,128)S(1)}, u32[]{:S(2)}, u32[]{:S(2)}) collective-permute-start(f32[16,6,128]{2,1,0:T(8,128)} %get-tuple-element.3), channel_id=1, source_target_pairs={{0,1},{1,2},{2,3},{3,4},{4,5},{5,6},{6,7},{7,8},{8,9},{9,10},{10,1... | collective-permute-start | bytes 147464 | tf_op jit(solution)/shard_map/ppermute | solution.py:144
  23.5 1.9 %collective-permute-start.1 = (f32[16,6,128]{2,1,0:T(8,128)S(1)}, f32[16,6,128]{2,1,0:T(8,128)S(1)}, u32[]{:S(2)}, u32[]{:S(2)}) collective-permute-start(f32[16,6,128]{2,1,0:T(8,128)S(1)} %get-tuple-element.2), channel_id=1, source_target_pairs={{1,0},{2,1},{3,2},{4,3},{5,4},{6,5},{7,6},{8,7},{9,8},{10,9},{11,1... | collective-permute-start | bytes 147464 | tf_op jit(solution)/shard_map/ppermute | solution.py:145
  25.5 0.1 copy.32
  25.6 0.1 reshape.51
  25.7 0.1 copy.28
  25.8 1.1 all-to-all-done
  26.9 1.8 %copy.30 = bf16[32,8,2,256]{3,2,0,1:T(2,128)(2,1)} copy(bf16[32,8,2,256]{3,2,1,0:T(2,128)(2,1)} %all-to-all-done) | data formatting | bytes 524288 | tf_op jit(solution)/shard_map/all_to_all | solution.py:157
  28.7 8.2 %all-to-all-start.1 = ((bf16[32,8,2,256]{3,2,0,1:T(2,128)(2,1)}), bf16[32,8,2,256]{3,2,0,1:T(2,128)(2,1)}, u32[]{:S(2)}, u32[]{:S(2)}) async-start(bf16[32,8,2,256]{3,2,0,1:T(2,128)(2,1)} %copy.30), calls=%async_computation.1 | async-start | bytes 524288 | tf_op jit(solution)/shard_map/all_to_all | solution.py:156
  36.9 53.8 %shard_map.86 = f32[3,256,128]{2,1,0:T(8,128)} custom-call(s32[8,256]{1,0:T(8,128)S(1)} %bitcast.11, f32[16,6,128]{2,1,0:T(8,128)S(1)} %collective-permute-done.before_ref, f32[256,6,128]{2,1,0:T(8,128)S(1)} %copy.34.mine_ref, f32[16,6,128]{2,1,0:T(8,128)S(1)} %collective-permute-done.1.after_ref), custom_call_target="tpu_custom_call" | custom-call | flops 60000002048 | bytes 2000000 | tf_op jit(solution)/shard_map/pallas_call | solution.py:121
  90.7 1.1 copy.31
  91.9 0.1 reshape.40
  92.0 17.0 %gather_fusion.1 = bf16[4096,256]{1,0:T(8,128)(2,1)} fusion(bf16[512,256]{1,0:T(8,128)(2,1)S(1)} %reshape.40, s32[4096]{0:T(1024)S(1)} %broadcast_clamp_fusion), kind=kCustom, calls=%fused_computation.1 | custom fusion | bytes 4210688 | tf_op jit(solution)/shard_map/gather | solution.py:164
  109.0 2.3 %fusion.3 = bf16[256,16,256]{2,1,0:T(8,128)(2,1)S(1)} fusion(bf16[256,16,256]{2,1,0:T(8,128)(2,1)} %bitcast.12, s32[256,16]{1,0:T(8,128)S(1)} %copy.28), kind=kOutput, calls=%fused_computation.6 | convolution fusion | flops 34668544 | bytes 4210688 | tf_op jit(solution)/shard_map/lnt,lnq->ltq/dot_general | solution.py:166
  111.3 2.0 %fusion.4 = f32[256,256]{1,0:T(8,128)} fusion(bf16[16,256,256]{2,1,0:T(8,128)(2,1)S(1)} %copy-done, bf16[256,16,256]{2,1,0:T(8,128)(2,1)S(1)} %fusion.3), kind=kOutput, calls=%fused_computation.7 | convolution fusion | flops 536870912 | bytes 4456448 | tf_op jit(solution)/shard_map/ltq,tqp->lp/dot_general | solution.py:167
  (12 shorter events, 0.0 us)
Async XLA Ops:
  0.6 110.7 %copy-start = (bf16[16,256,256]{2,1,0:T(8,128)(2,1)S(1)}, bf16[16,256,256]{2,1,0:T(8,128)(2,1)}, u32[]{:S(2)}) copy-start(bf16[16,256,256]{2,1,0:T(8,128)(2,1)} %param.8) | copy-start | bytes 6291460
  4.3 21.2 %copy-start.3 = (s32[256,16]{0,1:T(8,128)S(1)}, s32[256,16]{0,1:T(8,128)}, u32[]{:S(2)}) copy-start(s32[256,16]{0,1:T(8,128)} %param.10) | copy-start | bytes 49156
  4.3 21.4 %copy-start.2 = (s32[256,16]{0,1:T(8,128)S(1)}, s32[256,16]{0,1:T(8,128)}, u32[]{:S(2)}) copy-start(s32[256,16]{0,1:T(8,128)} %param.11) | copy-start | bytes 49156
  5.1 31.8 %copy-start.1 = (s32[256,8]{0,1:T(8,128)S(1)}, s32[256,8]{0,1:T(8,128)}, u32[]{:S(2)}) copy-start(s32[256,8]{0,1:T(8,128)} %param.12) | copy-start | bytes 24580
  5.1 21.8 %all-to-all-start = ((bf16[32,8,2,256]{3,2,1,0:T(2,128)(2,1)}), bf16[32,8,2,256]{3,2,1,0:T(2,128)(2,1)}, u32[]{:S(2)}, u32[]{:S(2)}) async-start(bf16[32,8,2,256]{3,2,1,0:T(2,128)(2,1)} %reshape.39), calls=%async_computation | async-start | bytes 524288 | tf_op jit(solution)/shard_map/all_to_all | solution.py:157
  19.5 17.4 %collective-permute-start = (f32[16,6,128]{2,1,0:T(8,128)}, f32[16,6,128]{2,1,0:T(8,128)S(1)}, u32[]{:S(2)}, u32[]{:S(2)}) collective-permute-start(f32[16,6,128]{2,1,0:T(8,128)} %get-tuple-element.3), channel_id=1, source_target_pairs={{0,1},{1,2},{2,3},{3,4},{4,5},{5,6},{6,7},{7,8},{8,9},{9,10},{10,1... | collective-permute-start | bytes 147464 | tf_op jit(solution)/shard_map/ppermute | solution.py:144
  23.5 13.4 %collective-permute-start.1 = (f32[16,6,128]{2,1,0:T(8,128)S(1)}, f32[16,6,128]{2,1,0:T(8,128)S(1)}, u32[]{:S(2)}, u32[]{:S(2)}) collective-permute-start(f32[16,6,128]{2,1,0:T(8,128)S(1)} %get-tuple-element.2), channel_id=1, source_target_pairs={{1,0},{2,1},{3,2},{4,3},{5,4},{6,5},{7,6},{8,7},{9,8},{10,9},{11,1... | collective-permute-start | bytes 147464 | tf_op jit(solution)/shard_map/ppermute | solution.py:145
  28.7 62.0 %all-to-all-start.1 = ((bf16[32,8,2,256]{3,2,0,1:T(2,128)(2,1)}), bf16[32,8,2,256]{3,2,0,1:T(2,128)(2,1)}, u32[]{:S(2)}, u32[]{:S(2)}) async-start(bf16[32,8,2,256]{3,2,0,1:T(2,128)(2,1)} %copy.30), calls=%async_computation.1 | async-start | bytes 524288 | tf_op jit(solution)/shard_map/all_to_all | solution.py:156

commit v2 on v1

v2 whole, which is shorter than its diff:
```python
import functools
import math

import jax
import jax.numpy as jnp
from jax import lax
from jax.experimental import pallas as pl
from jax.experimental.pallas import tpu as pltpu
from jax.sharding import PartitionSpec as P

Q = 256
P_SIZE = 128
NT = 16
NL = 16
NN = 8
CAP = 2
HALO = 16
EPS2 = 0.25
NLF = 256
NE = NLF + 2 * HALO
UNROLL = 4
bf = jnp.bfloat16
f32 = jnp.float32


def split3(v):
    a=v.astype(bf).astype(f32); r=v-a
    b=r.astype(bf).astype(f32)
    return a,b,r-b

def near_kernel(near_ref, before_ref, mine_ref, after_ref, out_ref, tgt, bt, gb, wa, wb, acc, *, U, PU):
    rows=lax.broadcasted_iota(jnp.int32,(8,128),0)
    lane=lax.broadcasted_iota(jnp.int32,(1,128),1)
    z8=jnp.zeros((8,128),f32)
    lo3=rows<3; lo6=rows<6; is6=rows==6
    is0=(rows==0)|(rows==3); is1=(rows==1)|(rows==4)
    keep=[((lane>=32*v)&(lane<32*v+32)).astype(f32).astype(bf) for v in range(4)]
    def one(ref,e,eg):
        y=[jnp.broadcast_to(ref[c,pl.ds(e,1),:],(8,128)) for c in range(6)]
        y,f=y[:3],y[3:]
        n=y[0]*y[0]+y[1]*y[1]+y[2]*y[2]
        a=y[0]*f[0]+y[1]*f[1]+y[2]*f[2]
        Q=jnp.where(is0,y[0],jnp.where(is1,y[1],y[2]))
        F=jnp.where(is0,f[0],jnp.where(is1,f[1],f[2]))
        t0=jnp.where(lo3,n*F+a*Q,jnp.where(lo6,F,jnp.where(is6,a,y[2]*f[2])))
        t1=jnp.where(lo3,y[0],jnp.where(lo6,y[1],y[2]))*jnp.where(lo6,F,jnp.where(is6,f[0],f[1]))
        t=jnp.concatenate([t0,t1],axis=0)
        g1=t.astype(bf)
        g2=(t-g1.astype(f32)).astype(bf)
        gb[eg]=jnp.concatenate([g1,g2],axis=0)
        q1,q2,q3=split3(Q)
        m=split3(n+EPS2)
        M=[jnp.where(is6,v,1.0) for v in m]
        src=jnp.concatenate([jnp.where(lo6,q1,M[0]),jnp.where(lo3,q1,jnp.where(lo6,q2,M[1])),jnp.where(lo3,q2,jnp.where(lo6,q3,M[2])),z8],axis=0)
        if ref is mine_ref:
            nn=split3(n)
            Nn=[jnp.where(is6,1.0,v) for v in nn]
            d1,d2,d3=-2.0*q1,-2.0*q2,-2.0*q3
            tg=jnp.concatenate([jnp.where(lo3,d1,jnp.where(lo6,d2,Nn[0])),jnp.where(lo3,d3,jnp.where(lo6,d1,Nn[1])),jnp.where(lo3,d2,jnp.where(lo6,d1,Nn[2])),z8],axis=0)
            tgt[e]=tg.astype(bf)
        return src.astype(bf)
    def prep(ref,base,n,un):
        def four(i,_):
            for w in range(un):
                o=(i*un+w)*4
                B=jnp.concatenate([one(ref,o+v,base+o+v) for v in range(4)],axis=0).T
                for v in range(4):
                    bt[base+o+v]=B*keep[v]
            return 0
        lax.fori_loop(0,n//(4*un),four,0)
    prep(before_ref,0,16,2); prep(mine_ref,16,256,PU); prep(after_ref,272,16,2)
    Z=jnp.zeros((128,128),bf)
    def stage1(l,w,u):
        A=tgt[l]
        A4=jnp.concatenate([A,A,A,A],axis=0)
        R=jnp.concatenate([jnp.concatenate([A4,Z],axis=1),jnp.concatenate([Z,A4],axis=1)],axis=0)
        D=[]
        for p in range(NN//2):
            k1=near_ref[2*p,l]; k2=near_ref[2*p+1,l]
            D.append(jnp.concatenate([bt[k1],bt[k2]],axis=1))
        s=jnp.dot(jnp.concatenate(D,axis=0),R,preferred_element_type=f32)
        v=lax.rsqrt(s)
        w3=(v*v*v).astype(bf)
        for p in range(NN//2):
            w[u,p*256:p*256+128,:]=w3[p*128:p*128+128,:128]
            w[u,p*256+128:p*256+256,:]=w3[p*128:p*128+128,128:]
    def stage2(l,w,u):
        G=jnp.concatenate([gb[near_ref[k,l]] for k in range(NN)],axis=1)
        T=jnp.dot(G,w[u],preferred_element_type=f32)
        acc[pl.ds(pl.multiple_of(l*16,16),16),:]=T[0:16]+T[16:32]
    for u in range(U): stage1(u,wa,u)
    def it(i,_):
        b=i*2*U
        for u in range(U):
            stage1(b+U+u,wb,u)
            stage2(b+u,wa,u)
        for u in range(U):
            stage1(jnp.minimum(b+2*U+u,NLF-1),wa,u)
            stage2(b+U+u,wb,u)
        return 0
    lax.fori_loop(0,NLF//(2*U),it,0)
    scale=1.0/(8.0*math.pi)
    def fin(g,_):
        x=[mine_ref[c,pl.ds(g*8,8),:] for c in range(3)]
        t=[acc[pl.ds(g*8*16+r,8,stride=16),:] for r in range(16)]
        n=x[0]*x[0]+x[1]*x[1]+x[2]*x[2]+2*EPS2
        N=t[0:3]; F=t[3:6]; A=t[6]
        Ym=[t[8:11],t[11:14],[t[14],t[15],t[7]]]
        xf=x[0]*F[0]+x[1]*F[1]+x[2]*F[2]-A
        for c in range(3):
            v=n*F[c]+N[c]+x[c]*xf
            for b in range(3):
                v=v-x[b]*(2.0*Ym[b][c]+Ym[c][b])
            out_ref[c,pl.ds(g*8,8),:]=v*scale
        return 0
    lax.fori_loop(0,32,fin,0)

def near(near_list, before, mine, after):
    return pl.pallas_call(
        functools.partial(near_kernel, U=UNROLL, PU=4),
        out_shape=jax.ShapeDtypeStruct((3, NLF, P_SIZE), f32),
        in_specs=[pl.BlockSpec(memory_space=pltpu.SMEM)] + [pl.BlockSpec(memory_space=pltpu.VMEM)] * 3,
        out_specs=pl.BlockSpec(memory_space=pltpu.VMEM),
        scratch_shapes=[
            pltpu.VMEM((NLF, 32, 128), bf),
            pltpu.VMEM((NE, 128, 128), bf),
            pltpu.VMEM((NE, 32, 128), bf),
            pltpu.VMEM((UNROLL, 1024, 128), bf),
            pltpu.VMEM((UNROLL, 1024, 128), bf),
            pltpu.VMEM((NLF * 16, 128), f32),
        ],
        compiler_params=pltpu.CompilerParams(vmem_limit_bytes=48 * 2**20),
        cost_estimate=pl.CostEstimate(flops=60 * 10**9, bytes_accessed=2 * 10**6, transcendentals=33 * 10**6),
    )(near_list.T, before, mine, after)


def far_kernel(enc_ref, r_ref, t_ref, out_ref, g_ref):
    sub = lax.broadcasted_iota(jnp.int32, (256, 256), 0)
    leaf = lax.broadcasted_iota(jnp.int32, (1, 256), 1) // NL
    lane = lax.broadcasted_iota(jnp.int32, (1, 512), 1).astype(f32)
    def block(b, _):
        e = enc_ref[pl.ds(b, 1), :]
        slot = (e & 511).astype(f32)
        cls = (e >> 9) * 16 + leaf
        col = jnp.concatenate([jnp.broadcast_to(slot[:, h * 128 : h * 128 + 128], (128, 128)).T for h in range(2)], axis=0)
        col = jnp.concatenate([col] * 4, axis=1)
        pick = (col == lane).astype(f32).astype(bf)
        rows = jnp.dot(pick, r_ref[...], preferred_element_type=f32).astype(bf)
        own = (sub == cls).astype(f32).astype(bf)
        g = jnp.dot(own, rows, preferred_element_type=f32).astype(bf)
        for t in range(NT):
            g_ref[t, pl.ds(pl.multiple_of(b * 16, 16), 16), :] = g[t * 16 : t * 16 + 16]
        return 0
    lax.fori_loop(0, 16, block, 0, unroll=2)
    acc = jnp.dot(g_ref[0], t_ref[0], preferred_element_type=f32)
    for t in range(1, NT):
        acc = acc + jnp.dot(g_ref[t], t_ref[t], preferred_element_type=f32)
    out_ref[...] = acc


def far(enc, received, translations):
    return pl.pallas_call(far_kernel, out_shape=jax.ShapeDtypeStruct((256,Q),f32),
        in_specs=[pl.BlockSpec(memory_space=pltpu.VMEM)]*3, out_specs=pl.BlockSpec(memory_space=pltpu.VMEM),
        scratch_shapes=[pltpu.VMEM((NT,256,Q),bf)],
        compiler_params=pltpu.CompilerParams(vmem_limit_bytes=24*2**20))(enc,received,translations)


def halo(x, axes):
    devices = lax.axis_size(axes)
    odd = lax.axis_index(axes) % 2 == 1
    leading, last = x[:, :HALO], x[:, x.shape[1] - HALO :]
    first = [(i, i ^ 1) for i in range(devices)]
    second = [(i, i + 1) for i in range(1, devices - 1, 2)]
    second += [(j, i) for i, j in second]
    one = lax.ppermute(jnp.where(odd, leading, last), axes, first)
    two = lax.ppermute(jnp.where(odd, last, leading), axes, second)
    return jnp.where(odd, one, two), jnp.where(odd, two, one)


def body(multipoles, translations, send_index, far_slots, far_types, near_list, particles):
    axes = ("gx", "gy", "gz")
    devices = send_index.shape[1]
    mine = jnp.transpose(particles, (1, 0, 2))
    before, after = halo(mine, axes)
    outgoing = multipoles[send_index[0]].reshape(devices, CAP * Q // 128, 128)
    incoming = lax.all_to_all(outgoing, axes, split_axis=0, concat_axis=0, tiled=True)
    entries = (far_slots + devices * CAP * far_types).reshape(16, NLF * NL // 16)
    speeds = near(near_list, before, mine, after)
    expansion = far(entries, incoming.reshape(devices * CAP, Q), translations)
    return (expansion, jnp.transpose(speeds, (1, 0, 2)))


def solution(mesh):
    placed = (
        P(("gx", "gy", "gz"), None),
        P(),
        P(("gx", "gy", "gz"), None, None),
        P(("gx", "gy", "gz"), None),
        P(("gx", "gy", "gz"), None),
        P(("gx", "gy", "gz"), None),
        P(("gx", "gy", "gz"), None, None),
    )
    return jax.shard_map(
        body,
        mesh=mesh,
        in_specs=placed,
        out_specs=(P(("gx", "gy", "gz"), None), P(("gx", "gy", "gz"), None, None)),
        check_vma=False,
    )
```

time: 114 us -> 72.4 us (0.64)
  local copies, waits for them, and re-layouts: 26.2 us -> 3.41 us
  starting transfers between devices: 26.3 us -> 19 us
  Pallas kernels: 53.8 us -> 47.4 us
  matrix products: 4.3 us -> 0 us
    gather x2 -> x1, local copies, waits for them, and re-layouts: 19.5 us -> 1.95 us  [body(): outgoing = multipoles[send_index[0]].reshape(devices, CAP * Q // 128, 128)]
    pallas_call x1 -> x2, Pallas kernels: 53.8 us -> 47.4 us  [the longest x1 39.3 us: near(): pl.pallas_call(functools.partial(near_kernel, U=UNROLL, PU=4), out_shape=...]
    all_to_all x2 -> x1, starting transfers between devices: 20.3 us -> 14.4 us  [body(): lax.all_to_all(outgoing, axes, split_axis=0, concat_axis=0, tiled=True)]
    dot_general x2 -> x0, matrix products: 4.3 us -> none  [the longest x1 2.28 us: body(): jnp.einsum('lnt,lnq->ltq', onehot, rows, preferred_element_type=f32)]
    all_to_all x2 -> x0, local copies, waits for them, and re-layouts: 2.96 us -> none  [the longest x1 1.83 us: body(): lax.all_to_all(outgoing, ('gx', 'gy'), split_axis=0, concat_axis=0, tiled...]
    unnamed x10 -> x12, local copies, waits for them, and re-layouts: 1.74 us -> 0.04 us
    ppermute x2, starting transfers between devices: 5.95 us -> 4.68 us  [the longest x1 4.59 us: halo(): two = lax.ppermute(jnp.where(odd, last, leading), axes, second)]
  transfers between devices with their start and end apart: 4 -> 3, of which waited for: 1 -> 0; matrix products, arithmetic and copies ran while one was open for 4% -> 5% of each run, Pallas kernels for 47% -> 54%
where the time goes in v2:
time: 72.4 us; the launch traced here: 72.3 us
  Pallas kernels  47.4 us (65%)
  starting transfers between devices  19 us (26%)
  local copies, waits for them, and re-layouts  3.41 us (5%)
  other arithmetic  1.59 us (2%)
  between operations  0.83 us (1%)
    pallas_call x1, Pallas kernels, near(): pl.pallas_call(functools.partial(near_kernel, U=UNROLL, PU=4), out_shape=...  39.3 us
    all_to_all x1, starting transfers between devices, body(): lax.all_to_all(outgoing, axes, split_axis=0, concat_axis=0, tiled=True)  14.4 us
    pallas_call x1, Pallas kernels, far(): pl.pallas_call(far_kernel, out_shape=jax.ShapeDtypeStruct((256, Q), f32),...  8.06 us
    ppermute x1, starting transfers between devices, halo(): two = lax.ppermute(jnp.where(odd, last, leading), axes, second)  4.59 us
    gather x1, local copies, waits for them, and re-layouts, body(): outgoing = multipoles[send_index[0]].reshape(devices, CAP * Q // 128, 128)  1.95 us
  transfers between devices with their start and end apart: 3, of which 0 were waited for; matrix products, arithmetic and copies ran while one was open for 5% of the time, Pallas kernels for 54%

profile of v2, /device:TPU:1, one launch (start us, length us, event | category | flops | bytes accessed | tf_op | source)
XLA Modules:
  0.0 72.3 jit_solution(5429499791393824997)
XLA Ops:
  0.6 0.0 copy-start
  0.6 0.0 copy-start.5
  0.7 0.0 copy-start.4
  0.7 0.9 %slice_select_fusion = (f32[6,16,128]{2,1,0:T(8,128)S(1)}, f32[6,16,128]{2,1,0:T(8,128)S(1)}) fusion(f32[6,256,128]{2,1,0:T(8,128)} %bitcast.7, pred[]{:T(512)S(6)} %eq.5), kind=kLoop, calls=%fused_computation.1 | loop fusion | flops 24576 | bytes 196609 | tf_op jit(solution)/shard_map/jit(_where)/select_n | solution.py:176
  1.6 4.6 %collective-permute-start.1 = (f32[6,16,128]{2,1,0:T(8,128)S(1)}, f32[6,16,128]{2,1,0:T(8,128)S(1)}, u32[]{:S(2)}, u32[]{:S(2)}) collective-permute-start(f32[6,16,128]{2,1,0:T(8,128)S(1)} %get-tuple-element.2), channel_id=1, source_target_pairs={{1,2},{3,4},{5,6},{7,8},{9,10},{11,12},{13,14},{15,16},{17,18},{19... | collective-permute-start | bytes 147464 | tf_op jit(solution)/shard_map/ppermute | solution.py:176
  6.2 0.1 collective-permute-start
  6.3 0.7 compare_select_fusion
  6.9 0.1 copy.11
  7.1 0.0 copy-start.2
  7.1 0.0 copy-start.3
  7.1 0.1 reshape.46
  7.3 0.0 copy-done
  7.3 2.0 %gather_fusion = bf16[512,256]{1,0:T(8,128)(2,1)S(1)} fusion(bf16[256,256]{1,0:T(8,128)(2,1)S(1)} %copy-done, s32[1024]{0:T(1024)S(1)} %pad_clamp_fusion), kind=kCustom, calls=%fused_computation | custom fusion | bytes 526336 | tf_op jit(solution)/shard_map/gather | solution.py:185
  9.2 0.8 %reshape.42 = bf16[256,4,128]{2,1,0:T(4,128)(2,1)} reshape(bf16[512,256]{1,0:T(8,128)(2,1)S(1)} %gather_fusion) | data formatting | bytes 524288 | tf_op jit(solution)/shard_map/reshape | solution.py:185
  10.0 14.4 %all-to-all-start = ((bf16[256,4,128]{2,1,0:T(4,128)(2,1)}), bf16[256,4,128]{2,1,0:T(4,128)(2,1)S(1)}, u32[]{:S(2)}, u32[]{:S(2)}) async-start(bf16[256,4,128]{2,1,0:T(4,128)(2,1)} %reshape.42), calls=%async_computation | async-start | bytes 524288 | tf_op jit(solution)/shard_map/all_to_all | solution.py:186
  24.4 0.1 copy.10
  24.5 0.1 reshape.41.enc_ref
  24.6 0.0 collective-permute-done.1
  24.6 0.0 collective-permute-done
  24.7 0.0 copy-start.1
  24.7 39.3 %shard_map.87 = f32[3,256,128]{2,1,0:T(8,128)} custom-call(s32[8,256]{1,0:T(8,128)S(1)} %bitcast.9, f32[6,16,128]{2,1,0:T(8,128)S(1)} %get-tuple-element.5.before_ref, f32[6,256,128]{2,1,0:T(8,128)S(1)} %bitcast.8, f32[6,16,128]{2,1,0:T(8,128)S(1)} %get-tuple-element.4.after_ref), custom_call_target="tpu_custom_call" | custom-call | flops 60000002048 | bytes 2000000 | tf_op jit(solution)/shard_map/pallas_call | solution.py:119
  64.0 0.0 all-to-all-done
  64.0 0.2 reshape.43.r_ref
  64.2 8.1 %shard_map.86 = f32[256,256]{1,0:T(8,128)} custom-call(s32[16,256]{1,0:T(8,128)S(1)} %reshape.41.enc_ref, bf16[512,256]{1,0:T(8,128)(2,1)S(1)} %reshape.43.r_ref, bf16[16,256,256]{2,1,0:T(8,128)(2,1)S(1)} %copy-done.1), custom_call_target="tpu_custom_call" | custom-call | tf_op jit(solution)/shard_map/pallas_call | solution.py:162
  (8 shorter events, 0.0 us)
Async XLA Ops:
  0.6 6.6 %copy-start = (bf16[256,256]{1,0:T(8,128)(2,1)S(1)}, bf16[256,256]{1,0:T(8,128)(2,1)}, u32[]{:S(2)}) copy-start(bf16[256,256]{1,0:T(8,128)(2,1)} %param.7) | copy-start | bytes 393220
  0.6 23.7 %copy-start.5 = (s32[256,16]{0,1:T(8,128)S(1)}, s32[256,16]{0,1:T(8,128)}, u32[]{:S(2)}) copy-start(s32[256,16]{0,1:T(8,128)} %param.11) | copy-start | bytes 49156
  0.7 23.7 %copy-start.4 = (s32[256,16]{0,1:T(8,128)S(1)}, s32[256,16]{0,1:T(8,128)}, u32[]{:S(2)}) copy-start(s32[256,16]{0,1:T(8,128)} %param.10) | copy-start | bytes 49156
  1.6 23.1 %collective-permute-start.1 = (f32[6,16,128]{2,1,0:T(8,128)S(1)}, f32[6,16,128]{2,1,0:T(8,128)S(1)}, u32[]{:S(2)}, u32[]{:S(2)}) collective-permute-start(f32[6,16,128]{2,1,0:T(8,128)S(1)} %get-tuple-element.2), channel_id=1, source_target_pairs={{1,2},{3,4},{5,6},{7,8},{9,10},{11,12},{13,14},{15,16},{17,18},{19... | collective-permute-start | bytes 147464 | tf_op jit(solution)/shard_map/ppermute | solution.py:176
  6.2 18.5 %collective-permute-start = (f32[6,16,128]{2,1,0:T(8,128)S(1)}, f32[6,16,128]{2,1,0:T(8,128)S(1)}, u32[]{:S(2)}, u32[]{:S(2)}) collective-permute-start(f32[6,16,128]{2,1,0:T(8,128)S(1)} %get-tuple-element.3), channel_id=1, source_target_pairs={{0,1},{1,0},{2,3},{3,2},{4,5},{5,4},{6,7},{7,6},{8,9},{9,8},{10,11... | collective-permute-start | bytes 147464 | tf_op jit(solution)/shard_map/ppermute | solution.py:175
  7.1 17.6 %copy-start.2 = (f32[256,6,128]{2,0,1:T(8,128)S(1)}, f32[256,6,128]{2,0,1:T(8,128)}, u32[]{:S(2)}) copy-start(f32[256,6,128]{2,0,1:T(8,128)} %param.13) | copy-start | bytes 2359300
  7.1 17.6 %copy-start.3 = (s32[256,8]{0,1:T(8,128)S(1)}, s32[256,8]{0,1:T(8,128)}, u32[]{:S(2)}) copy-start(s32[256,8]{0,1:T(8,128)} %param.12) | copy-start | bytes 24580
  10.0 54.0 %all-to-all-start = ((bf16[256,4,128]{2,1,0:T(4,128)(2,1)}), bf16[256,4,128]{2,1,0:T(4,128)(2,1)S(1)}, u32[]{:S(2)}, u32[]{:S(2)}) async-start(bf16[256,4,128]{2,1,0:T(4,128)(2,1)} %reshape.42), calls=%async_computation | async-start | bytes 524288 | tf_op jit(solution)/shard_map/all_to_all | solution.py:186
  24.7 39.5 %copy-start.1 = (bf16[16,256,256]{2,1,0:T(8,128)(2,1)S(1)}, bf16[16,256,256]{2,1,0:T(8,128)(2,1)}, u32[]{:S(2)}) copy-start(bf16[16,256,256]{2,1,0:T(8,128)(2,1)} %t_ref.1) | copy-start | bytes 6291460

commit v3 on v2

--- a/solution.py
+++ b/solution.py
@@ -19,6 +19,7 @@
 NLF = 256
 NE = NLF + 2 * HALO
 UNROLL = 4
+BLOCKS = 8
 bf = jnp.bfloat16
 f32 = jnp.float32
 
@@ -28,13 +29,17 @@
     b=r.astype(bf).astype(f32)
     return a,b,r-b
 
-def near_kernel(near_ref, before_ref, mine_ref, after_ref, out_ref, tgt, bt, gb, wa, wb, acc, *, U, PU):
+def near_kernel(near_hbm, before_ref, mine_hbm, after_ref, out_ref, tgt, bt, gb, wa, wb, acc, mine_ref, near_ref, sems, *, U, PU):
+    copies=[pltpu.make_async_copy(mine_hbm,mine_ref,sems.at[0]),pltpu.make_async_copy(near_hbm,near_ref,sems.at[1])]
+    for copy in copies: copy.start()
     rows=lax.broadcasted_iota(jnp.int32,(8,128),0)
     lane=lax.broadcasted_iota(jnp.int32,(1,128),1)
     z8=jnp.zeros((8,128),f32)
     lo3=rows<3; lo6=rows<6; is6=rows==6
     is0=(rows==0)|(rows==3); is1=(rows==1)|(rows==4)
     keep=[((lane>=32*v)&(lane<32*v+32)).astype(f32).astype(bf) for v in range(4)]
+    is7=rows==7; end=lo3|is7
+    scale_t=jnp.where(lo6,-2.0,jnp.where(is6,0.0,1.0)); fixed_t=jnp.where(is6,1.0,0.0)
     def one(ref,e,eg):
         y=[jnp.broadcast_to(ref[c,pl.ds(e,1),:],(8,128)) for c in range(6)]
         y,f=y[:3],y[3:]
@@ -48,16 +53,11 @@
         g1=t.astype(bf)
         g2=(t-g1.astype(f32)).astype(bf)
         gb[eg]=jnp.concatenate([g1,g2],axis=0)
-        q1,q2,q3=split3(Q)
-        m=split3(n+EPS2)
-        M=[jnp.where(is6,v,1.0) for v in m]
-        src=jnp.concatenate([jnp.where(lo6,q1,M[0]),jnp.where(lo3,q1,jnp.where(lo6,q2,M[1])),jnp.where(lo3,q2,jnp.where(lo6,q3,M[2])),z8],axis=0)
+        q1,q2,q3=split3(jnp.where(lo6,Q,jnp.where(is6,n+EPS2,n)))
+        src=jnp.concatenate([jnp.where(is7,1.0,q1),jnp.where(is7,1.0,jnp.where(lo3,q1,q2)),jnp.where(is7,1.0,jnp.where(lo3,q2,q3)),z8],axis=0)
         if ref is mine_ref:
-            nn=split3(n)
-            Nn=[jnp.where(is6,1.0,v) for v in nn]
-            d1,d2,d3=-2.0*q1,-2.0*q2,-2.0*q3
-            tg=jnp.concatenate([jnp.where(lo3,d1,jnp.where(lo6,d2,Nn[0])),jnp.where(lo3,d3,jnp.where(lo6,d1,Nn[1])),jnp.where(lo3,d2,jnp.where(lo6,d1,Nn[2])),z8],axis=0)
-            tgt[e]=tg.astype(bf)
+            tg=[jnp.where(end,q1,q2),jnp.where(lo3,q3,jnp.where(is7,q2,q1)),jnp.where(lo3,q2,jnp.where(is7,q3,q1))]
+            tgt[e]=jnp.concatenate([v*scale_t+fixed_t for v in tg]+[z8],axis=0).astype(bf)
         return src.astype(bf)
     def prep(ref,base,n,un):
         def four(i,_):
@@ -68,7 +68,9 @@
                     bt[base+o+v]=B*keep[v]
             return 0
         lax.fori_loop(0,n//(4*un),four,0)
-    prep(before_ref,0,16,2); prep(mine_ref,16,256,PU); prep(after_ref,272,16,2)
+    prep(before_ref,0,16,4); prep(after_ref,272,16,4)
+    for copy in copies: copy.wait()
+    prep(mine_ref,16,256,PU)
     Z=jnp.zeros((128,128),bf)
     def stage1(l,w,u):
         A=tgt[l]
@@ -89,16 +91,6 @@
         T=jnp.dot(G,w[u],preferred_element_type=f32)
         acc[pl.ds(pl.multiple_of(l*16,16),16),:]=T[0:16]+T[16:32]
     for u in range(U): stage1(u,wa,u)
-    def it(i,_):
-        b=i*2*U
-        for u in range(U):
-            stage1(b+U+u,wb,u)
-            stage2(b+u,wa,u)
-        for u in range(U):
-            stage1(jnp.minimum(b+2*U+u,NLF-1),wa,u)
-            stage2(b+U+u,wb,u)
-        return 0
-    lax.fori_loop(0,NLF//(2*U),it,0)
     scale=1.0/(8.0*math.pi)
     def fin(g,_):
         x=[mine_ref[c,pl.ds(g*8,8),:] for c in range(3)]
@@ -113,13 +105,24 @@
                 v=v-x[b]*(2.0*Ym[b][c]+Ym[c][b])
             out_ref[c,pl.ds(g*8,8),:]=v*scale
         return 0
-    lax.fori_loop(0,32,fin,0)
+    def it(i,_):
+        b=i*2*U
+        fin(jnp.maximum(i-1,0),0)
+        for u in range(U):
+            stage1(b+U+u,wb,u)
+            stage2(b+u,wa,u)
+        for u in range(U):
+            stage1(jnp.minimum(b+2*U+u,NLF-1),wa,u)
+            stage2(b+U+u,wb,u)
+        return 0
+    lax.fori_loop(0,NLF//(2*U),it,0)
+    fin(NLF//8-1,0)
 
 def near(near_list, before, mine, after):
     return pl.pallas_call(
         functools.partial(near_kernel, U=UNROLL, PU=4),
         out_shape=jax.ShapeDtypeStruct((3, NLF, P_SIZE), f32),
-        in_specs=[pl.BlockSpec(memory_space=pltpu.SMEM)] + [pl.BlockSpec(memory_space=pltpu.VMEM)] * 3,
+        in_specs=[pl.BlockSpec(memory_space=m) for m in (pltpu.HBM, pltpu.VMEM, pltpu.HBM, pltpu.VMEM)],
         out_specs=pl.BlockSpec(memory_space=pltpu.VMEM),
         scratch_shapes=[
             pltpu.VMEM((NLF, 32, 128), bf),
@@ -128,41 +131,71 @@
             pltpu.VMEM((UNROLL, 1024, 128), bf),
             pltpu.VMEM((UNROLL, 1024, 128), bf),
             pltpu.VMEM((NLF * 16, 128), f32),
+            pltpu.VMEM((6, NLF, 128), f32),
+            pltpu.SMEM((NN, NLF), jnp.int32),
+            pltpu.SemaphoreType.DMA((2,)),
         ],
-        compiler_params=pltpu.CompilerParams(vmem_limit_bytes=48 * 2**20),
+        compiler_params=pltpu.CompilerParams(vmem_limit_bytes=32 * 2**20),
         cost_estimate=pl.CostEstimate(flops=60 * 10**9, bytes_accessed=2 * 10**6, transcendentals=33 * 10**6),
     )(near_list.T, before, mine, after)
 
 
-def far_kernel(enc_ref, r_ref, t_ref, out_ref, g_ref):
+def far_kernel(enc_ref, r_ref, t_ref, out_ref, g_ref, s_ref):
+    s_ref[...] = r_ref[...].reshape(1024, 128).astype(f32)
+    table = jnp.concatenate([s_ref[pl.ds(h, 512, stride=2), :] for h in range(2)], axis=1).astype(bf)
     sub = lax.broadcasted_iota(jnp.int32, (256, 256), 0)
     leaf = lax.broadcasted_iota(jnp.int32, (1, 256), 1) // NL
     lane = lax.broadcasted_iota(jnp.int32, (1, 512), 1).astype(f32)
-    def block(b, _):
+    def picks(b):
         e = enc_ref[pl.ds(b, 1), :]
         slot = (e & 511).astype(f32)
         cls = (e >> 9) * 16 + leaf
         col = jnp.concatenate([jnp.broadcast_to(slot[:, h * 128 : h * 128 + 128], (128, 128)).T for h in range(2)], axis=0)
         col = jnp.concatenate([col] * 4, axis=1)
         pick = (col == lane).astype(f32).astype(bf)
-        rows = jnp.dot(pick, r_ref[...], preferred_element_type=f32).astype(bf)
         own = (sub == cls).astype(f32).astype(bf)
-        g = jnp.dot(own, rows, preferred_element_type=f32).astype(bf)
-        for t in range(NT):
-            g_ref[t, pl.ds(pl.multiple_of(b * 16, 16), 16), :] = g[t * 16 : t * 16 + 16]
+        return pick, own
+    def block(i, _):
+        both = [picks(i * BLOCKS + j) for j in range(BLOCKS)]
+        rows = jnp.dot(jnp.concatenate([p for p, _ in both], axis=0), table, preferred_element_type=f32).astype(bf)
+        for j in range(BLOCKS):
+            g = jnp.dot(both[j][1], rows[j * 256 : j * 256 + 256], preferred_element_type=f32).astype(bf)
+            b = pl.multiple_of((i * BLOCKS + j) * 16, 16)
+            for t in range(NT):
+                g_ref[pl.ds(b, 16), t * Q : t * Q + Q] = g[t * 16 : t * 16 + 16]
         return 0
-    lax.fori_loop(0, 16, block, 0, unroll=2)
-    acc = jnp.dot(g_ref[0], t_ref[0], preferred_element_type=f32)
-    for t in range(1, NT):
-        acc = acc + jnp.dot(g_ref[t], t_ref[t], preferred_element_type=f32)
-    out_ref[...] = acc
+    lax.fori_loop(0, 16 // BLOCKS, block, 0)
+    out_ref[...] = jnp.dot(g_ref[...], t_ref[...].reshape(NT * Q, Q), preferred_element_type=f32)
 
 
 def far(enc, received, translations):
     return pl.pallas_call(far_kernel, out_shape=jax.ShapeDtypeStruct((256,Q),f32),
         in_specs=[pl.BlockSpec(memory_space=pltpu.VMEM)]*3, out_specs=pl.BlockSpec(memory_space=pltpu.VMEM),
-        scratch_shapes=[pltpu.VMEM((NT,256,Q),bf)],
+        scratch_shapes=[pltpu.VMEM((256,NT*Q),bf), pltpu.VMEM((1024,128),f32)],
         compiler_params=pltpu.CompilerParams(vmem_limit_bytes=24*2**20))(enc,received,translations)
+
+
+def pick_kernel(i_ref, m_ref, out_ref, rows_ref):
+    lane = lax.broadcasted_iota(jnp.int32, (1, 256), 1).astype(f32)
+    for c in range(2):
+        index = i_ref[c : c + 1, :].astype(f32)
+        col = jnp.concatenate([jnp.broadcast_to(index[:, h * 128 : h * 128 + 128], (128, 128)).T for h in range(2)], axis=0)
+        pick = (jnp.concatenate([col, col], axis=1) == lane).astype(f32).astype(bf)
+        got = jnp.dot(pick, m_ref[...], preferred_element_type=f32)
+        for h in range(2):
+            rows_ref[pl.ds(2 * c + h, 256, stride=4), :] = got[:, h * 128 : h * 128 + 128]
+    out_ref[...] = rows_ref[...].astype(bf).reshape(256, 4, 128)
+
+
+def pick(index, m):
+    return pl.pallas_call(
+        pick_kernel,
+        out_shape=jax.ShapeDtypeStruct((256, 4, 128), bf),
+        in_specs=[pl.BlockSpec(memory_space=pltpu.VMEM)] * 2,
+        out_specs=pl.BlockSpec(memory_space=pltpu.VMEM),
+        scratch_shapes=[pltpu.VMEM((1024, 128), f32)],
+        cost_estimate=pl.CostEstimate(flops=4 * 10**9, bytes_accessed=10**7, transcendentals=0),
+    )(index, m)
 
 
 def halo(x, axes):
@@ -182,11 +215,11 @@
     devices = send_index.shape[1]
     mine = jnp.transpose(particles, (1, 0, 2))
     before, after = halo(mine, axes)
-    outgoing = multipoles[send_index[0]].reshape(devices, CAP * Q // 128, 128)
+    outgoing = pick(send_index[0].T, multipoles)
     incoming = lax.all_to_all(outgoing, axes, split_axis=0, concat_axis=0, tiled=True)
     entries = (far_slots + devices * CAP * far_types).reshape(16, NLF * NL // 16)
     speeds = near(near_list, before, mine, after)
-    expansion = far(entries, incoming.reshape(devices * CAP, Q), translations)
+    expansion = far(entries, incoming, translations)
     return (expansion, jnp.transpose(speeds, (1, 0, 2)))
 
 

time: 72.4 us -> 65.4 us (0.903)
  local copies, waits for them, and re-layouts: 3.41 us -> 0.24 us
  Pallas kernels: 47.4 us -> 44.3 us
  other arithmetic: 1.59 us -> 0.86 us
    pallas_call x1, Pallas kernels: 8.06 us -> 3.96 us  [far(): pl.pallas_call(far_kernel, out_shape=jax.ShapeDtypeStruct((256, Q), f32),...]
    pallas_call x0 -> x1, Pallas kernels: none -> 2.02 us  [pick(): pl.pallas_call(pick_kernel, out_shape=jax.ShapeDtypeStruct((256, 4, 128),...]
    gather x1 -> x0, local copies, waits for them, and re-layouts: 1.95 us -> none  [body(): outgoing = multipoles[send_index[0]].reshape(devices, CAP * Q // 128, 128)]
    pallas_call x1, Pallas kernels: 39.3 us -> 38.3 us  [near(): pl.pallas_call(functools.partial(near_kernel, U=UNROLL, PU=4), out_shape=...]
    reshape x2 -> x0, local copies, waits for them, and re-layouts: 0.94 us -> none  [the longest x1 0.77 us: body(): outgoing = multipoles[send_index[0]].reshape(devices, CAP * Q // 128, 128)]
  transfers between devices with their start and end apart: 3 -> 3, of which waited for: 0 -> 0; matrix products, arithmetic and copies ran while one was open for 5% -> 0% of each run, Pallas kernels for 54% -> 62%
where the time goes in v3:
time: 65.4 us; the launch traced here: 65.2 us
  Pallas kernels  44.3 us (68%)
  starting transfers between devices  19 us (29%)
  other arithmetic  0.86 us (1%)
  between operations  0.8 us (1%)
    pallas_call x1, Pallas kernels, near(): pl.pallas_call(functools.partial(near_kernel, U=UNROLL, PU=4), out_shape=...  38.3 us
    all_to_all x1, starting transfers between devices, body(): lax.all_to_all(outgoing, axes, split_axis=0, concat_axis=0, tiled=True)  14.3 us
    ppermute x1, starting transfers between devices, halo(): two = lax.ppermute(jnp.where(odd, last, leading), axes, second)  4.59 us
    pallas_call x1, Pallas kernels, far(): pl.pallas_call(far_kernel, out_shape=jax.ShapeDtypeStruct((256, Q), f32),...  3.96 us
    pallas_call x1, Pallas kernels, pick(): pl.pallas_call(pick_kernel, out_shape=jax.ShapeDtypeStruct((256, 4, 128),...  2.02 us
  transfers between devices with their start and end apart: 3, of which 0 were waited for; matrix products, arithmetic and copies ran while one was open for 0% of the time, Pallas kernels for 62%

profile of v3, /device:TPU:1, one launch (start us, length us, event | category | flops | bytes accessed | tf_op | source)
XLA Modules:
  0.0 65.2 jit_solution(1097031962436486736)
XLA Ops:
  0.6 0.8 %slice_select_fusion = (f32[6,16,128]{2,1,0:T(8,128)S(1)}, f32[6,16,128]{2,1,0:T(8,128)S(1)}) fusion(f32[6,256,128]{2,1,0:T(8,128)} %bitcast.6, pred[]{:T(512)S(6)} %eq.5), kind=kLoop, calls=%fused_computation | loop fusion | flops 24576 | bytes 196609 | tf_op jit(solution)/shard_map/jit(_where)/select_n | solution.py:209
  1.5 4.6 %collective-permute-start.1 = (f32[6,16,128]{2,1,0:T(8,128)S(1)}, f32[6,16,128]{2,1,0:T(8,128)S(1)}, u32[]{:S(2)}, u32[]{:S(2)}) collective-permute-start(f32[6,16,128]{2,1,0:T(8,128)S(1)} %get-tuple-element.2), channel_id=1, source_target_pairs={{1,2},{3,4},{5,6},{7,8},{9,10},{11,12},{13,14},{15,16},{17,18},{19... | collective-permute-start | bytes 147464 | tf_op jit(solution)/shard_map/ppermute | solution.py:209
  6.1 0.1 collective-permute-start
  6.2 0.0 copy-start.3
  6.2 0.0 copy-start.4
  6.2 0.0 copy-start.1
  6.2 0.0 copy-start.2
  6.2 2.0 %shard_map.86 = bf16[256,4,128]{2,1,0:T(4,128)(2,1)} custom-call(s32[2,256]{1,0:T(2,128)} %bitcast.9, bf16[256,256]{1,0:T(8,128)(2,1)} %m_ref.1), custom_call_target="tpu_custom_call" | custom-call | flops 4000000000 | bytes 10000000 | tf_op jit(solution)/shard_map/pallas_call | solution.py:191
  8.3 14.3 %all-to-all-start = ((bf16[256,4,128]{2,1,0:T(4,128)(2,1)}), bf16[256,4,128]{2,1,0:T(4,128)(2,1)S(1)}, u32[]{:S(2)}, u32[]{:S(2)}) async-start(bf16[256,4,128]{2,1,0:T(4,128)(2,1)} %shard_map.86), calls=%async_computation | async-start | bytes 524288 | tf_op jit(solution)/shard_map/all_to_all | solution.py:219
  22.6 0.0 copy-done.3
  22.6 0.0 copy-done.4
  22.6 0.1 copy.10
  22.7 0.1 reshape.7.enc_ref
  22.8 0.0 collective-permute-done.1
  22.8 0.0 collective-permute-done
  22.9 0.0 copy-done.1
  22.9 0.0 copy-done.2
  22.9 0.0 copy-start
  22.9 38.3 %shard_map.88 = f32[3,256,128]{2,1,0:T(8,128)} custom-call(s32[8,256]{1,0:T(8,128)S(1)} %bitcast.8, f32[6,16,128]{2,1,0:T(8,128)S(1)} %get-tuple-element.5.before_ref, f32[6,256,128]{2,1,0:T(8,128)S(1)} %bitcast.7, f32[6,16,128]{2,1,0:T(8,128)S(1)} %get-tuple-element.4.after_ref), custom_call_target="tpu_custom_call" | custom-call | flops 60000002048 | bytes 2000000 | tf_op jit(solution)/shard_map/pallas_call | solution.py:122
  61.2 0.0 all-to-all-done.r_ref
  61.2 0.0 copy-done
  61.3 4.0 %shard_map.87 = f32[256,256]{1,0:T(8,128)} custom-call(s32[16,256]{1,0:T(8,128)S(1)} %reshape.7.enc_ref, bf16[256,4,128]{2,1,0:T(4,128)(2,1)S(1)} %all-to-all-done.r_ref, bf16[16,256,256]{2,1,0:T(8,128)(2,1)S(1)} %copy-done), custom_call_target="tpu_custom_call" | custom-call | tf_op jit(solution)/shard_map/pallas_call | solution.py:172
  (2 shorter events, 0.0 us)
Async XLA Ops:
  1.5 21.3 %collective-permute-start.1 = (f32[6,16,128]{2,1,0:T(8,128)S(1)}, f32[6,16,128]{2,1,0:T(8,128)S(1)}, u32[]{:S(2)}, u32[]{:S(2)}) collective-permute-start(f32[6,16,128]{2,1,0:T(8,128)S(1)} %get-tuple-element.2), channel_id=1, source_target_pairs={{1,2},{3,4},{5,6},{7,8},{9,10},{11,12},{13,14},{15,16},{17,18},{19... | collective-permute-start | bytes 147464 | tf_op jit(solution)/shard_map/ppermute | solution.py:209
  6.1 16.8 %collective-permute-start = (f32[6,16,128]{2,1,0:T(8,128)S(1)}, f32[6,16,128]{2,1,0:T(8,128)S(1)}, u32[]{:S(2)}, u32[]{:S(2)}) collective-permute-start(f32[6,16,128]{2,1,0:T(8,128)S(1)} %get-tuple-element.3), channel_id=1, source_target_pairs={{0,1},{1,0},{2,3},{3,2},{4,5},{5,4},{6,7},{7,6},{8,9},{9,8},{10,11... | collective-permute-start | bytes 147464 | tf_op jit(solution)/shard_map/ppermute | solution.py:208
  6.2 16.4 %copy-start.3 = (s32[256,16]{0,1:T(8,128)S(1)}, s32[256,16]{0,1:T(8,128)}, u32[]{:S(2)}) copy-start(s32[256,16]{0,1:T(8,128)} %param.10) | copy-start | bytes 49156
  6.2 16.4 %copy-start.4 = (s32[256,16]{0,1:T(8,128)S(1)}, s32[256,16]{0,1:T(8,128)}, u32[]{:S(2)}) copy-start(s32[256,16]{0,1:T(8,128)} %param.11) | copy-start | bytes 49156
  6.2 16.7 %copy-start.1 = (f32[256,6,128]{2,0,1:T(8,128)S(1)}, f32[256,6,128]{2,0,1:T(8,128)}, u32[]{:S(2)}) copy-start(f32[256,6,128]{2,0,1:T(8,128)} %param.13) | copy-start | bytes 2359300
  6.2 16.7 %copy-start.2 = (s32[256,8]{0,1:T(8,128)S(1)}, s32[256,8]{0,1:T(8,128)}, u32[]{:S(2)}) copy-start(s32[256,8]{0,1:T(8,128)} %param.12) | copy-start | bytes 24580
  8.3 53.0 %all-to-all-start = ((bf16[256,4,128]{2,1,0:T(4,128)(2,1)}), bf16[256,4,128]{2,1,0:T(4,128)(2,1)S(1)}, u32[]{:S(2)}, u32[]{:S(2)}) async-start(bf16[256,4,128]{2,1,0:T(4,128)(2,1)} %shard_map.86), calls=%async_computation | async-start | bytes 524288 | tf_op jit(solution)/shard_map/all_to_all | solution.py:219
  22.9 38.4 %copy-start = (bf16[16,256,256]{2,1,0:T(8,128)(2,1)S(1)}, bf16[16,256,256]{2,1,0:T(8,128)(2,1)}, u32[]{:S(2)}) copy-start(bf16[16,256,256]{2,1,0:T(8,128)(2,1)} %t_ref.1) | copy-start | bytes 6291460

commit v4 on v3

--- a/solution.py
+++ b/solution.py
@@ -18,7 +18,7 @@
 EPS2 = 0.25
 NLF = 256
 NE = NLF + 2 * HALO
-UNROLL = 4
+UNROLL = 16
 BLOCKS = 8
 bf = jnp.bfloat16
 f32 = jnp.float32
@@ -73,24 +73,19 @@
     prep(mine_ref,16,256,PU)
     Z=jnp.zeros((128,128),bf)
     def stage1(l,w,u):
-        A=tgt[l]
-        A4=jnp.concatenate([A,A,A,A],axis=0)
-        R=jnp.concatenate([jnp.concatenate([A4,Z],axis=1),jnp.concatenate([Z,A4],axis=1)],axis=0)
-        D=[]
-        for p in range(NN//2):
-            k1=near_ref[2*p,l]; k2=near_ref[2*p+1,l]
-            D.append(jnp.concatenate([bt[k1],bt[k2]],axis=1))
+        A4,B4=[jnp.concatenate([tgt[l+j]]*4,axis=0) for j in range(2)]
+        R=jnp.concatenate([jnp.concatenate([A4,Z],axis=1),jnp.concatenate([Z,B4],axis=1)],axis=0)
+        D=[jnp.concatenate([bt[near_ref[k,l+j]] for j in range(2)],axis=1) for k in range(NN)]
         s=jnp.dot(jnp.concatenate(D,axis=0),R,preferred_element_type=f32)
         v=lax.rsqrt(s)
         w3=(v*v*v).astype(bf)
-        for p in range(NN//2):
-            w[u,p*256:p*256+128,:]=w3[p*128:p*128+128,:128]
-            w[u,p*256+128:p*256+256,:]=w3[p*128:p*128+128,128:]
+        for j in range(2):
+            w[u+j]=w3[:,j*128:j*128+128]
     def stage2(l,w,u):
         G=jnp.concatenate([gb[near_ref[k,l]] for k in range(NN)],axis=1)
         T=jnp.dot(G,w[u],preferred_element_type=f32)
         acc[pl.ds(pl.multiple_of(l*16,16),16),:]=T[0:16]+T[16:32]
-    for u in range(U): stage1(u,wa,u)
+    for u in range(0,U,2): stage1(u,wa,u)
     scale=1.0/(8.0*math.pi)
     def fin(g,_):
         x=[mine_ref[c,pl.ds(g*8,8),:] for c in range(3)]
@@ -107,16 +102,18 @@
         return 0
     def it(i,_):
         b=i*2*U
-        fin(jnp.maximum(i-1,0),0)
-        for u in range(U):
+        for j in range(2*U//8): fin(jnp.maximum(i-1,0)*(2*U//8)+j,0)
+        for u in range(0,U,2):
             stage1(b+U+u,wb,u)
             stage2(b+u,wa,u)
-        for u in range(U):
-            stage1(jnp.minimum(b+2*U+u,NLF-1),wa,u)
+            stage2(b+u+1,wa,u+1)
+        for u in range(0,U,2):
+            stage1(jnp.minimum(b+2*U+u,NLF-2),wa,u)
             stage2(b+U+u,wb,u)
+            stage2(b+U+u+1,wb,u+1)
         return 0
     lax.fori_loop(0,NLF//(2*U),it,0)
-    fin(NLF//8-1,0)
+    for j in range(2*U//8): fin(NLF//8-2*U//8+j,0)
 
 def near(near_list, before, mine, after):
     return pl.pallas_call(

time: 65.4 us -> 62 us (0.948)
  Pallas kernels: 44.3 us -> 40.9 us
    pallas_call x1, Pallas kernels: 38.3 us -> 34.9 us  [near(): pl.pallas_call(functools.partial(near_kernel, U=UNROLL, PU=4), out_shape=...]
  transfers between devices with their start and end apart: 3 -> 3, of which waited for: 0 -> 0; matrix products, arithmetic and copies ran while one was open for 0% -> 0% of each run, Pallas kernels for 62% -> 60%
where the time goes in v4:
time: 62 us; the launch traced here: 61.8 us
  Pallas kernels  40.9 us (66%)
  starting transfers between devices  19 us (31%)
  other arithmetic  0.86 us (1%)
  between operations  0.8 us (1%)
    pallas_call x1, Pallas kernels, near(): pl.pallas_call(functools.partial(near_kernel, U=UNROLL, PU=4), out_shape=...  34.9 us
    all_to_all x1, starting transfers between devices, body(): lax.all_to_all(outgoing, axes, split_axis=0, concat_axis=0, tiled=True)  14.3 us
    ppermute x1, starting transfers between devices, halo(): two = lax.ppermute(jnp.where(odd, last, leading), axes, second)  4.59 us
    pallas_call x1, Pallas kernels, far(): pl.pallas_call(far_kernel, out_shape=jax.ShapeDtypeStruct((256, Q), f32),...  3.96 us
    pallas_call x1, Pallas kernels, pick(): pl.pallas_call(pick_kernel, out_shape=jax.ShapeDtypeStruct((256, 4, 128),...  2.02 us
  transfers between devices with their start and end apart: 3, of which 0 were waited for; matrix products, arithmetic and copies ran while one was open for 0% of the time, Pallas kernels for 60%

profile of v4, /device:TPU:1, one launch (start us, length us, event | category | flops | bytes accessed | tf_op | source)
XLA Modules:
  0.0 61.8 jit_solution(12820325472829602830)
XLA Ops:
  0.6 0.8 %slice_select_fusion = (f32[6,16,128]{2,1,0:T(8,128)S(1)}, f32[6,16,128]{2,1,0:T(8,128)S(1)}) fusion(f32[6,256,128]{2,1,0:T(8,128)} %bitcast.6, pred[]{:T(512)S(6)} %eq.5), kind=kLoop, calls=%fused_computation | loop fusion | flops 24576 | bytes 196609 | tf_op jit(solution)/shard_map/jit(_where)/select_n | solution.py:206
  1.5 4.6 %collective-permute-start.1 = (f32[6,16,128]{2,1,0:T(8,128)S(1)}, f32[6,16,128]{2,1,0:T(8,128)S(1)}, u32[]{:S(2)}, u32[]{:S(2)}) collective-permute-start(f32[6,16,128]{2,1,0:T(8,128)S(1)} %get-tuple-element.2), channel_id=1, source_target_pairs={{1,2},{3,4},{5,6},{7,8},{9,10},{11,12},{13,14},{15,16},{17,18},{19... | collective-permute-start | bytes 147464 | tf_op jit(solution)/shard_map/ppermute | solution.py:206
  6.1 0.1 collective-permute-start
  6.2 0.0 copy-start.3
  6.2 0.0 copy-start.4
  6.2 0.0 copy-start.1
  6.2 0.0 copy-start.2
  6.2 2.0 %shard_map.86 = bf16[256,4,128]{2,1,0:T(4,128)(2,1)} custom-call(s32[2,256]{1,0:T(2,128)} %bitcast.9, bf16[256,256]{1,0:T(8,128)(2,1)} %m_ref.1), custom_call_target="tpu_custom_call" | custom-call | flops 4000000000 | bytes 10000000 | tf_op jit(solution)/shard_map/pallas_call | solution.py:188
  8.3 14.3 %all-to-all-start = ((bf16[256,4,128]{2,1,0:T(4,128)(2,1)}), bf16[256,4,128]{2,1,0:T(4,128)(2,1)S(1)}, u32[]{:S(2)}, u32[]{:S(2)}) async-start(bf16[256,4,128]{2,1,0:T(4,128)(2,1)} %shard_map.86), calls=%async_computation | async-start | bytes 524288 | tf_op jit(solution)/shard_map/all_to_all | solution.py:216
  22.6 0.0 copy-done.3
  22.6 0.0 copy-done.4
  22.6 0.1 copy.10
  22.7 0.1 reshape.7.enc_ref
  22.8 0.0 collective-permute-done.1
  22.8 0.0 collective-permute-done
  22.9 0.0 copy-done.1
  22.9 0.0 copy-done.2
  22.9 0.0 copy-start
  22.9 34.9 %shard_map.88 = f32[3,256,128]{2,1,0:T(8,128)} custom-call(s32[8,256]{1,0:T(8,128)S(1)} %bitcast.8, f32[6,16,128]{2,1,0:T(8,128)S(1)} %get-tuple-element.5.before_ref, f32[6,256,128]{2,1,0:T(8,128)S(1)} %bitcast.7, f32[6,16,128]{2,1,0:T(8,128)S(1)} %get-tuple-element.4.after_ref), custom_call_target="tpu_custom_call" | custom-call | flops 60000002048 | bytes 2000000 | tf_op jit(solution)/shard_map/pallas_call | solution.py:119
  57.8 0.0 all-to-all-done.r_ref
  57.8 0.0 copy-done
  57.8 4.0 %shard_map.87 = f32[256,256]{1,0:T(8,128)} custom-call(s32[16,256]{1,0:T(8,128)S(1)} %reshape.7.enc_ref, bf16[256,4,128]{2,1,0:T(4,128)(2,1)S(1)} %all-to-all-done.r_ref, bf16[16,256,256]{2,1,0:T(8,128)(2,1)S(1)} %copy-done), custom_call_target="tpu_custom_call" | custom-call | tf_op jit(solution)/shard_map/pallas_call | solution.py:169
  (2 shorter events, 0.0 us)
Async XLA Ops:
  1.5 21.3 %collective-permute-start.1 = (f32[6,16,128]{2,1,0:T(8,128)S(1)}, f32[6,16,128]{2,1,0:T(8,128)S(1)}, u32[]{:S(2)}, u32[]{:S(2)}) collective-permute-start(f32[6,16,128]{2,1,0:T(8,128)S(1)} %get-tuple-element.2), channel_id=1, source_target_pairs={{1,2},{3,4},{5,6},{7,8},{9,10},{11,12},{13,14},{15,16},{17,18},{19... | collective-permute-start | bytes 147464 | tf_op jit(solution)/shard_map/ppermute | solution.py:206
  6.1 16.8 %collective-permute-start = (f32[6,16,128]{2,1,0:T(8,128)S(1)}, f32[6,16,128]{2,1,0:T(8,128)S(1)}, u32[]{:S(2)}, u32[]{:S(2)}) collective-permute-start(f32[6,16,128]{2,1,0:T(8,128)S(1)} %get-tuple-element.3), channel_id=1, source_target_pairs={{0,1},{1,0},{2,3},{3,2},{4,5},{5,4},{6,7},{7,6},{8,9},{9,8},{10,11... | collective-permute-start | bytes 147464 | tf_op jit(solution)/shard_map/ppermute | solution.py:205
  6.2 16.4 %copy-start.3 = (s32[256,16]{0,1:T(8,128)S(1)}, s32[256,16]{0,1:T(8,128)}, u32[]{:S(2)}) copy-start(s32[256,16]{0,1:T(8,128)} %param.10) | copy-start | bytes 49156
  6.2 16.4 %copy-start.4 = (s32[256,16]{0,1:T(8,128)S(1)}, s32[256,16]{0,1:T(8,128)}, u32[]{:S(2)}) copy-start(s32[256,16]{0,1:T(8,128)} %param.11) | copy-start | bytes 49156
  6.2 16.7 %copy-start.1 = (f32[256,6,128]{2,0,1:T(8,128)S(1)}, f32[256,6,128]{2,0,1:T(8,128)}, u32[]{:S(2)}) copy-start(f32[256,6,128]{2,0,1:T(8,128)} %param.13) | copy-start | bytes 2359300
  6.2 16.7 %copy-start.2 = (s32[256,8]{0,1:T(8,128)S(1)}, s32[256,8]{0,1:T(8,128)}, u32[]{:S(2)}) copy-start(s32[256,8]{0,1:T(8,128)} %param.12) | copy-start | bytes 24580
  8.3 49.5 %all-to-all-start = ((bf16[256,4,128]{2,1,0:T(4,128)(2,1)}), bf16[256,4,128]{2,1,0:T(4,128)(2,1)S(1)}, u32[]{:S(2)}, u32[]{:S(2)}) async-start(bf16[256,4,128]{2,1,0:T(4,128)(2,1)} %shard_map.86), calls=%async_computation | async-start | bytes 524288 | tf_op jit(solution)/shard_map/all_to_all | solution.py:216
  22.9 34.9 %copy-start = (bf16[16,256,256]{2,1,0:T(8,128)(2,1)S(1)}, bf16[16,256,256]{2,1,0:T(8,128)(2,1)}, u32[]{:S(2)}) copy-start(bf16[16,256,256]{2,1,0:T(8,128)(2,1)} %t_ref.1) | copy-start | bytes 6291460

commit v5 on v4

--- a/solution.py
+++ b/solution.py
@@ -102,14 +102,15 @@
         return 0
     def it(i,_):
         b=i*2*U
-        for j in range(2*U//8): fin(jnp.maximum(i-1,0)*(2*U//8)+j,0)
         for u in range(0,U,2):
+            if u%8==0: fin(jnp.maximum(i-1,0)*(2*U//8)+u//8,0)
+            stage2(b+u,wa,u)
             stage1(b+U+u,wb,u)
-            stage2(b+u,wa,u)
             stage2(b+u+1,wa,u+1)
         for u in range(0,U,2):
+            if u%8==0: fin(jnp.maximum(i-1,0)*(2*U//8)+U//8+u//8,0)
+            stage2(b+U+u,wb,u)
             stage1(jnp.minimum(b+2*U+u,NLF-2),wa,u)
-            stage2(b+U+u,wb,u)
             stage2(b+U+u+1,wb,u+1)
         return 0
     lax.fori_loop(0,NLF//(2*U),it,0)
@@ -117,7 +118,7 @@
 
 def near(near_list, before, mine, after):
     return pl.pallas_call(
-        functools.partial(near_kernel, U=UNROLL, PU=4),
+        functools.partial(near_kernel, U=UNROLL, PU=8),
         out_shape=jax.ShapeDtypeStruct((3, NLF, P_SIZE), f32),
         in_specs=[pl.BlockSpec(memory_space=m) for m in (pltpu.HBM, pltpu.VMEM, pltpu.HBM, pltpu.VMEM)],
         out_specs=pl.BlockSpec(memory_space=pltpu.VMEM),

time: 62 us -> 61.5 us (level)
  transfers between devices with their start and end apart: 3 -> 3, of which waited for: 0 -> 0; matrix products, arithmetic and copies ran while one was open for 0% -> 0% of each run, Pallas kernels for 60% -> 59%
where the time goes in v5:
time: 61.5 us; the launch traced here: 61.3 us
  Pallas kernels  40.4 us (66%)
  starting transfers between devices  19 us (31%)
  other arithmetic  0.86 us (1%)
  between operations  0.8 us (1%)
    pallas_call x1, Pallas kernels, near(): pl.pallas_call(functools.partial(near_kernel, U=UNROLL, PU=8), out_shape=...  34.4 us
    all_to_all x1, starting transfers between devices, body(): lax.all_to_all(outgoing, axes, split_axis=0, concat_axis=0, tiled=True)  14.3 us
    ppermute x1, starting transfers between devices, halo(): two = lax.ppermute(jnp.where(odd, last, leading), axes, second)  4.59 us
    pallas_call x1, Pallas kernels, far(): pl.pallas_call(far_kernel, out_shape=jax.ShapeDtypeStruct((256, Q), f32),...  3.97 us
    pallas_call x1, Pallas kernels, pick(): pl.pallas_call(pick_kernel, out_shape=jax.ShapeDtypeStruct((256, 4, 128),...  2.02 us
  transfers between devices with their start and end apart: 3, of which 0 were waited for; matrix products, arithmetic and copies ran while one was open for 0% of the time, Pallas kernels for 59%

profile of v5, /device:TPU:1, one launch (start us, length us, event | category | flops | bytes accessed | tf_op | source)
XLA Modules:
  0.0 61.3 jit_solution(10321899821137504508)
XLA Ops:
  0.6 0.8 %slice_select_fusion = (f32[6,16,128]{2,1,0:T(8,128)S(1)}, f32[6,16,128]{2,1,0:T(8,128)S(1)}) fusion(f32[6,256,128]{2,1,0:T(8,128)} %bitcast.6, pred[]{:T(512)S(6)} %eq.5), kind=kLoop, calls=%fused_computation | loop fusion | flops 24576 | bytes 196609 | tf_op jit(solution)/shard_map/jit(_where)/select_n | solution.py:207
  1.5 4.6 %collective-permute-start.1 = (f32[6,16,128]{2,1,0:T(8,128)S(1)}, f32[6,16,128]{2,1,0:T(8,128)S(1)}, u32[]{:S(2)}, u32[]{:S(2)}) collective-permute-start(f32[6,16,128]{2,1,0:T(8,128)S(1)} %get-tuple-element.2), channel_id=1, source_target_pairs={{1,2},{3,4},{5,6},{7,8},{9,10},{11,12},{13,14},{15,16},{17,18},{19... | collective-permute-start | bytes 147464 | tf_op jit(solution)/shard_map/ppermute | solution.py:207
  6.1 0.1 collective-permute-start
  6.2 0.0 copy-start.3
  6.2 0.0 copy-start.4
  6.2 0.0 copy-start.1
  6.2 0.0 copy-start.2
  6.2 2.0 %shard_map.86 = bf16[256,4,128]{2,1,0:T(4,128)(2,1)} custom-call(s32[2,256]{1,0:T(2,128)} %bitcast.9, bf16[256,256]{1,0:T(8,128)(2,1)} %m_ref.1), custom_call_target="tpu_custom_call" | custom-call | flops 4000000000 | bytes 10000000 | tf_op jit(solution)/shard_map/pallas_call | solution.py:189
  8.3 14.3 %all-to-all-start = ((bf16[256,4,128]{2,1,0:T(4,128)(2,1)}), bf16[256,4,128]{2,1,0:T(4,128)(2,1)S(1)}, u32[]{:S(2)}, u32[]{:S(2)}) async-start(bf16[256,4,128]{2,1,0:T(4,128)(2,1)} %shard_map.86), calls=%async_computation | async-start | bytes 524288 | tf_op jit(solution)/shard_map/all_to_all | solution.py:217
  22.6 0.0 copy-done.3
  22.6 0.0 copy-done.4
  22.6 0.1 copy.10
  22.7 0.1 reshape.7.enc_ref
  22.8 0.0 collective-permute-done.1
  22.8 0.0 collective-permute-done
  22.9 0.0 copy-done.1
  22.9 0.0 copy-done.2
  22.9 0.0 copy-start
  22.9 34.4 %shard_map.88 = f32[3,256,128]{2,1,0:T(8,128)} custom-call(s32[8,256]{1,0:T(8,128)S(1)} %bitcast.8, f32[6,16,128]{2,1,0:T(8,128)S(1)} %get-tuple-element.5.before_ref, f32[6,256,128]{2,1,0:T(8,128)S(1)} %bitcast.7, f32[6,16,128]{2,1,0:T(8,128)S(1)} %get-tuple-element.4.after_ref), custom_call_target="tpu_custom_call" | custom-call | flops 60000002048 | bytes 2000000 | tf_op jit(solution)/shard_map/pallas_call | solution.py:120
  57.3 0.0 all-to-all-done.r_ref
  57.3 0.0 copy-done
  57.3 4.0 %shard_map.87 = f32[256,256]{1,0:T(8,128)} custom-call(s32[16,256]{1,0:T(8,128)S(1)} %reshape.7.enc_ref, bf16[256,4,128]{2,1,0:T(4,128)(2,1)S(1)} %all-to-all-done.r_ref, bf16[16,256,256]{2,1,0:T(8,128)(2,1)S(1)} %copy-done), custom_call_target="tpu_custom_call" | custom-call | tf_op jit(solution)/shard_map/pallas_call | solution.py:170
  (2 shorter events, 0.0 us)
Async XLA Ops:
  1.5 21.3 %collective-permute-start.1 = (f32[6,16,128]{2,1,0:T(8,128)S(1)}, f32[6,16,128]{2,1,0:T(8,128)S(1)}, u32[]{:S(2)}, u32[]{:S(2)}) collective-permute-start(f32[6,16,128]{2,1,0:T(8,128)S(1)} %get-tuple-element.2), channel_id=1, source_target_pairs={{1,2},{3,4},{5,6},{7,8},{9,10},{11,12},{13,14},{15,16},{17,18},{19... | collective-permute-start | bytes 147464 | tf_op jit(solution)/shard_map/ppermute | solution.py:207
  6.1 16.8 %collective-permute-start = (f32[6,16,128]{2,1,0:T(8,128)S(1)}, f32[6,16,128]{2,1,0:T(8,128)S(1)}, u32[]{:S(2)}, u32[]{:S(2)}) collective-permute-start(f32[6,16,128]{2,1,0:T(8,128)S(1)} %get-tuple-element.3), channel_id=1, source_target_pairs={{0,1},{1,0},{2,3},{3,2},{4,5},{5,4},{6,7},{7,6},{8,9},{9,8},{10,11... | collective-permute-start | bytes 147464 | tf_op jit(solution)/shard_map/ppermute | solution.py:206
  6.2 16.4 %copy-start.3 = (s32[256,16]{0,1:T(8,128)S(1)}, s32[256,16]{0,1:T(8,128)}, u32[]{:S(2)}) copy-start(s32[256,16]{0,1:T(8,128)} %param.10) | copy-start | bytes 49156
  6.2 16.4 %copy-start.4 = (s32[256,16]{0,1:T(8,128)S(1)}, s32[256,16]{0,1:T(8,128)}, u32[]{:S(2)}) copy-start(s32[256,16]{0,1:T(8,128)} %param.11) | copy-start | bytes 49156
  6.2 16.7 %copy-start.1 = (f32[256,6,128]{2,0,1:T(8,128)S(1)}, f32[256,6,128]{2,0,1:T(8,128)}, u32[]{:S(2)}) copy-start(f32[256,6,128]{2,0,1:T(8,128)} %param.13) | copy-start | bytes 2359300
  6.2 16.7 %copy-start.2 = (s32[256,8]{0,1:T(8,128)S(1)}, s32[256,8]{0,1:T(8,128)}, u32[]{:S(2)}) copy-start(s32[256,8]{0,1:T(8,128)} %param.12) | copy-start | bytes 24580
  8.3 49.0 %all-to-all-start = ((bf16[256,4,128]{2,1,0:T(4,128)(2,1)}), bf16[256,4,128]{2,1,0:T(4,128)(2,1)S(1)}, u32[]{:S(2)}, u32[]{:S(2)}) async-start(bf16[256,4,128]{2,1,0:T(4,128)(2,1)} %shard_map.86), calls=%async_computation | async-start | bytes 524288 | tf_op jit(solution)/shard_map/all_to_all | solution.py:217
  22.9 34.4 %copy-start = (bf16[16,256,256]{2,1,0:T(8,128)(2,1)S(1)}, bf16[16,256,256]{2,1,0:T(8,128)(2,1)}, u32[]{:S(2)}) copy-start(bf16[16,256,256]{2,1,0:T(8,128)(2,1)} %t_ref.1) | copy-start | bytes 6291460

commit v6 on v5

--- a/solution.py
+++ b/solution.py
@@ -18,7 +18,7 @@
 EPS2 = 0.25
 NLF = 256
 NE = NLF + 2 * HALO
-UNROLL = 16
+UNROLL = 32
 BLOCKS = 8
 bf = jnp.bfloat16
 f32 = jnp.float32
@@ -133,7 +133,7 @@
             pltpu.SMEM((NN, NLF), jnp.int32),
             pltpu.SemaphoreType.DMA((2,)),
         ],
-        compiler_params=pltpu.CompilerParams(vmem_limit_bytes=32 * 2**20),
+        compiler_params=pltpu.CompilerParams(vmem_limit_bytes=44 * 2**20),
         cost_estimate=pl.CostEstimate(flops=60 * 10**9, bytes_accessed=2 * 10**6, transcendentals=33 * 10**6),
     )(near_list.T, before, mine, after)
 

time: 61.5 us -> 62 us (level)
  transfers between devices with their start and end apart: 3 -> 3, of which waited for: 0 -> 0; matrix products, arithmetic and copies ran while one was open for 0% -> 0% of each run, Pallas kernels for 59% -> 60%
where the time goes in v6:
time: 62 us; the launch traced here: 61.8 us
  Pallas kernels  40.9 us (66%)
  starting transfers between devices  19 us (31%)
  other arithmetic  0.86 us (1%)
  between operations  0.8 us (1%)
    pallas_call x1, Pallas kernels, near(): pl.pallas_call(functools.partial(near_kernel, U=UNROLL, PU=8), out_shape=...  34.9 us
    all_to_all x1, starting transfers between devices, body(): lax.all_to_all(outgoing, axes, split_axis=0, concat_axis=0, tiled=True)  14.3 us
    ppermute x1, starting transfers between devices, halo(): two = lax.ppermute(jnp.where(odd, last, leading), axes, second)  4.59 us
    pallas_call x1, Pallas kernels, far(): pl.pallas_call(far_kernel, out_shape=jax.ShapeDtypeStruct((256, Q), f32),...  3.96 us
    pallas_call x1, Pallas kernels, pick(): pl.pallas_call(pick_kernel, out_shape=jax.ShapeDtypeStruct((256, 4, 128),...  2.02 us
  transfers between devices with their start and end apart: 3, of which 0 were waited for; matrix products, arithmetic and copies ran while one was open for 0% of the time, Pallas kernels for 60%

profile of v6, /device:TPU:1, one launch (start us, length us, event | category | flops | bytes accessed | tf_op | source)
XLA Modules:
  0.0 61.8 jit_solution(11041649016378878580)
XLA Ops:
  0.6 0.8 %slice_select_fusion = (f32[6,16,128]{2,1,0:T(8,128)S(1)}, f32[6,16,128]{2,1,0:T(8,128)S(1)}) fusion(f32[6,256,128]{2,1,0:T(8,128)} %bitcast.6, pred[]{:T(512)S(6)} %eq.5), kind=kLoop, calls=%fused_computation | loop fusion | flops 24576 | bytes 196609 | tf_op jit(solution)/shard_map/jit(_where)/select_n | solution.py:207
  1.5 4.6 %collective-permute-start.1 = (f32[6,16,128]{2,1,0:T(8,128)S(1)}, f32[6,16,128]{2,1,0:T(8,128)S(1)}, u32[]{:S(2)}, u32[]{:S(2)}) collective-permute-start(f32[6,16,128]{2,1,0:T(8,128)S(1)} %get-tuple-element.2), channel_id=1, source_target_pairs={{1,2},{3,4},{5,6},{7,8},{9,10},{11,12},{13,14},{15,16},{17,18},{19... | collective-permute-start | bytes 147464 | tf_op jit(solution)/shard_map/ppermute | solution.py:207
  6.1 0.1 collective-permute-start
  6.2 0.0 copy-start.3
  6.2 0.0 copy-start.4
  6.2 0.0 copy-start.1
  6.2 0.0 copy-start.2
  6.2 2.0 %shard_map.86 = bf16[256,4,128]{2,1,0:T(4,128)(2,1)} custom-call(s32[2,256]{1,0:T(2,128)} %bitcast.9, bf16[256,256]{1,0:T(8,128)(2,1)} %m_ref.1), custom_call_target="tpu_custom_call" | custom-call | flops 4000000000 | bytes 10000000 | tf_op jit(solution)/shard_map/pallas_call | solution.py:189
  8.3 14.3 %all-to-all-start = ((bf16[256,4,128]{2,1,0:T(4,128)(2,1)}), bf16[256,4,128]{2,1,0:T(4,128)(2,1)S(1)}, u32[]{:S(2)}, u32[]{:S(2)}) async-start(bf16[256,4,128]{2,1,0:T(4,128)(2,1)} %shard_map.86), calls=%async_computation | async-start | bytes 524288 | tf_op jit(solution)/shard_map/all_to_all | solution.py:217
  22.6 0.0 copy-done.3
  22.6 0.0 copy-done.4
  22.6 0.1 copy.10
  22.7 0.1 reshape.7.enc_ref
  22.8 0.0 collective-permute-done.1
  22.8 0.0 collective-permute-done
  22.9 0.0 copy-done.1
  22.9 0.0 copy-done.2
  22.9 0.0 copy-start
  22.9 34.9 %shard_map.88 = f32[3,256,128]{2,1,0:T(8,128)} custom-call(s32[8,256]{1,0:T(8,128)S(1)} %bitcast.8, f32[6,16,128]{2,1,0:T(8,128)S(1)} %get-tuple-element.5.before_ref, f32[6,256,128]{2,1,0:T(8,128)S(1)} %bitcast.7, f32[6,16,128]{2,1,0:T(8,128)S(1)} %get-tuple-element.4.after_ref), custom_call_target="tpu_custom_call" | custom-call | flops 60000002048 | bytes 2000000 | tf_op jit(solution)/shard_map/pallas_call | solution.py:120
  57.8 0.0 all-to-all-done.r_ref
  57.8 0.0 copy-done
  57.8 4.0 %shard_map.87 = f32[256,256]{1,0:T(8,128)} custom-call(s32[16,256]{1,0:T(8,128)S(1)} %reshape.7.enc_ref, bf16[256,4,128]{2,1,0:T(4,128)(2,1)S(1)} %all-to-all-done.r_ref, bf16[16,256,256]{2,1,0:T(8,128)(2,1)S(1)} %copy-done), custom_call_target="tpu_custom_call" | custom-call | tf_op jit(solution)/shard_map/pallas_call | solution.py:170
  (2 shorter events, 0.0 us)
Async XLA Ops:
  1.5 21.3 %collective-permute-start.1 = (f32[6,16,128]{2,1,0:T(8,128)S(1)}, f32[6,16,128]{2,1,0:T(8,128)S(1)}, u32[]{:S(2)}, u32[]{:S(2)}) collective-permute-start(f32[6,16,128]{2,1,0:T(8,128)S(1)} %get-tuple-element.2), channel_id=1, source_target_pairs={{1,2},{3,4},{5,6},{7,8},{9,10},{11,12},{13,14},{15,16},{17,18},{19... | collective-permute-start | bytes 147464 | tf_op jit(solution)/shard_map/ppermute | solution.py:207
  6.1 16.8 %collective-permute-start = (f32[6,16,128]{2,1,0:T(8,128)S(1)}, f32[6,16,128]{2,1,0:T(8,128)S(1)}, u32[]{:S(2)}, u32[]{:S(2)}) collective-permute-start(f32[6,16,128]{2,1,0:T(8,128)S(1)} %get-tuple-element.3), channel_id=1, source_target_pairs={{0,1},{1,0},{2,3},{3,2},{4,5},{5,4},{6,7},{7,6},{8,9},{9,8},{10,11... | collective-permute-start | bytes 147464 | tf_op jit(solution)/shard_map/ppermute | solution.py:206
  6.2 16.4 %copy-start.3 = (s32[256,16]{0,1:T(8,128)S(1)}, s32[256,16]{0,1:T(8,128)}, u32[]{:S(2)}) copy-start(s32[256,16]{0,1:T(8,128)} %param.10) | copy-start | bytes 49156
  6.2 16.4 %copy-start.4 = (s32[256,16]{0,1:T(8,128)S(1)}, s32[256,16]{0,1:T(8,128)}, u32[]{:S(2)}) copy-start(s32[256,16]{0,1:T(8,128)} %param.11) | copy-start | bytes 49156
  6.2 16.7 %copy-start.1 = (f32[256,6,128]{2,0,1:T(8,128)S(1)}, f32[256,6,128]{2,0,1:T(8,128)}, u32[]{:S(2)}) copy-start(f32[256,6,128]{2,0,1:T(8,128)} %param.13) | copy-start | bytes 2359300
  6.2 16.7 %copy-start.2 = (s32[256,8]{0,1:T(8,128)S(1)}, s32[256,8]{0,1:T(8,128)}, u32[]{:S(2)}) copy-start(s32[256,8]{0,1:T(8,128)} %param.12) | copy-start | bytes 24580
  8.3 49.6 %all-to-all-start = ((bf16[256,4,128]{2,1,0:T(4,128)(2,1)}), bf16[256,4,128]{2,1,0:T(4,128)(2,1)S(1)}, u32[]{:S(2)}, u32[]{:S(2)}) async-start(bf16[256,4,128]{2,1,0:T(4,128)(2,1)} %shard_map.86), calls=%async_computation | async-start | bytes 524288 | tf_op jit(solution)/shard_map/all_to_all | solution.py:217
  22.9 34.9 %copy-start = (bf16[16,256,256]{2,1,0:T(8,128)(2,1)S(1)}, bf16[16,256,256]{2,1,0:T(8,128)(2,1)}, u32[]{:S(2)}) copy-start(bf16[16,256,256]{2,1,0:T(8,128)(2,1)} %t_ref.1) | copy-start | bytes 6291460
